TPU v7x, 256 devices: a whole 4x4x8 slice. The times are simulated.
256 devices in a mesh: tm: 8 (over y, core), rows: 8 (over z), dp: 4 (over x).
Axes of the slice: x: 4, y: 4, z: 8, core: 2. Of those that a mesh axis runs over, the one named last changes fastest.
Arguments:
- video: bfloat16 [4, 128, 32, 32, 128], P('dp', 'tm', 'rows'), may hold values from -6 to 6
- cotangent: bfloat16 [4, 128, 32, 32, 128], P('dp', 'tm', 'rows'), may hold values from -6 to 6
- in_kernel: bfloat16 [3, 3, 128, 128], replicated, may hold values from -0.03125 to 0.03125
- out_kernel: bfloat16 [3, 3, 128, 128], replicated, may hold values from -0.1875 to 0.1875
- skip_gain: float32 [128], replicated, may hold values from 0.5 to 1.5
- log_decay: float32 [128, 128], P('tm'), may hold values from -3 to 0, as said below
Outputs:
- layer_out: bfloat16 [4, 128, 32, 32, 128], P('dp', 'tm', 'rows')
- video_grad: bfloat16 [4, 128, 32, 32, 128], P('dp', 'tm', 'rows')
- in_kernel_grad: float32 [3, 3, 128, 128], replicated
- out_kernel_grad: float32 [3, 3, 128, 128], replicated
- skip_gain_grad: float32 [128], replicated
- decay_grad: float32 [128, 128], P('tm')
Inputs may be any that keep to these rules, and one draw needn't show every extreme that they name: log_decay is negative.
All inputs are finite; a program needn't handle non-finite values.
Results may differ from a plain program's by a relative error of at most 0.0085.
Values may be sent and summed in bfloat16 or wider, within the bound.
A program may use at most 64 MiB of HBM per device.

v0:
```python
import math

import jax
import jax.numpy as jnp
from jax import lax
from jax.sharding import PartitionSpec as P


def padded_2(cells, sides, width):
    for axis, dim in sides:
        count = lax.axis_size(axis)
        ends = count - 1
        head = lax.slice_in_dim(cells, 0, width, axis=dim)
        tail = lax.slice_in_dim(cells, cells.shape[dim] - width, cells.shape[dim], axis=dim)
        cells = jnp.concatenate(
            [
                lax.ppermute(tail, axis, [(i, (i + 1) % count) for i in range(ends)]),
                cells,
                lax.ppermute(head, axis, [((i + 1) % count, i) for i in range(ends)]),
            ],
            axis=dim,
        )
    return cells


def prefix(value, axis, join, neutral):
    count, mine = (lax.axis_size(axis), lax.axis_index(axis))
    pieces = jax.tree.map(lambda part: lax.all_gather(part, axis), value)
    running = jax.tree.map(
        lambda part, zero: jnp.full_like(part, 0) + jnp.asarray(zero, part.dtype), value, neutral
    )

    def prefix_lap(position, running):
        longer = join(running, jax.tree.map(lambda part: part[position], pieces))
        return jax.tree.map(lambda new, old: jnp.where(position < mine, new, old), longer, running)

    return lax.fori_loop(0, count - 1, prefix_lap, running)


def entering(array, axis, combine, identity):
    devices, position = (lax.axis_size(axis), lax.axis_index(axis))
    everything = jax.tree.map(
        lambda part, kind: lax.all_gather(part.astype(kind), axis),
        array,
        (jnp.bfloat16, jnp.bfloat16),
    )
    start = jax.tree.map(
        lambda part, zero: jnp.broadcast_to(jnp.asarray(zero, part.dtype), part.shape),
        array,
        identity,
    )

    def entering_lap(k, before):
        at = devices - 1 - k
        reached = at > position
        new = combine(
            before, jax.tree.map(lambda part, own: part[at].astype(own.dtype), everything, array)
        )
        return jax.tree.map(lambda a, b: jnp.where(reached, a, b), new, before)

    return lax.fori_loop(0, devices, entering_lap, start)


def pad_columns(field):
    return jnp.pad(field, ((0, 0), (0, 0), (0, 0), (1, 1), (0, 0)))


def forward_conv(padded, kernel):
    seqs, frames, rows_two, cols_two, chans = padded.shape
    rows, cols = (rows_two - 2, cols_two - 2)
    total = None
    for i in range(3):
        for j in range(3):
            piece = padded[:, :, i : i + rows, j : j + cols, :].reshape(-1, chans)
            term = jnp.dot(piece, kernel[i, j], preferred_element_type=jnp.float32)
            total = term if total is None else total + term
    return total.reshape(seqs, frames, rows, cols, kernel.shape[3])


def adjoint_conv(padded, kernel):
    seqs, frames, rows_two, cols_two, chans = padded.shape
    rows, cols = (rows_two - 2, cols_two - 2)
    total = None
    for i in range(3):
        for j in range(3):
            piece = padded[:, :, 2 - i : 2 - i + rows, 2 - j : 2 - j + cols, :].reshape(-1, chans)
            term = lax.dot_general(
                piece, kernel[i, j], (((1,), (1,)), ((), ())), preferred_element_type=jnp.float32
            )
            total = term if total is None else total + term
    return total.reshape(seqs, frames, rows, cols, kernel.shape[2])


def kernel_grad(padded, grad):
    seqs, frames, rows_two, cols_two, chans = padded.shape
    rows, cols = (rows_two - 2, cols_two - 2)
    flat_grad = grad.reshape(-1, grad.shape[-1])
    outer_list = []
    for i in range(3):
        inner_list = []
        for j in range(3):
            piece = padded[:, :, i : i + rows, j : j + cols, :].reshape(-1, chans)
            inner_list.append(
                lax.dot_general(
                    piece, flat_grad, (((0,), (0,)), ((), ())), preferred_element_type=jnp.float32
                )
            )
        outer_list.append(jnp.stack(inner_list))
    return jnp.stack(outer_list)


def combine_groups(earlier, later):
    return (earlier[0] * later[0], later[0] * earlier[1] + later[1])


def on_device(video, cotangent, in_kernel, out_kernel, skip_gain, log_decay):
    seqs, frames, rows, cols, chans = video.shape
    padded_x = pad_columns(padded_2(video, (("rows", 2),), 1))
    drive = forward_conv(padded_x, in_kernel)
    cum = jnp.cumsum(log_decay, axis=0)
    later_mask = (
        lax.broadcasted_iota(jnp.int32, (frames, frames), 0)
        >= lax.broadcasted_iota(jnp.int32, (frames, frames), 1)
    )[:, :, None]
    gaps = cum[:, None, :] - cum[None, :, :]
    within = jnp.where(later_mask, jnp.exp(jnp.where(later_mask, gaps, 0.0)), 0.0)
    local_states = jnp.einsum("tkp,skrcp->strcp", within, drive, precision=lax.Precision.HIGHEST)
    group_total = cum[-1]
    group_decay = jnp.exp(group_total)
    empty = jnp.zeros_like(local_states[:, -1])
    identity = (jnp.ones_like(group_total), empty)
    _, carry_in = prefix((group_decay, local_states[:, -1]), "tm", combine_groups, identity)
    states = local_states + jnp.exp(cum)[None, :, None, None, :] * carry_in[:, None]
    states_bf = states.astype(jnp.bfloat16)
    padded_s = pad_columns(padded_2(states_bf, (("rows", 2),), 1))
    pre = forward_conv(padded_s, out_kernel) + skip_gain * video.astype(jnp.float32)
    activated, pullback = jax.vjp(jax.nn.gelu, pre)
    grad_pre = pullback(cotangent.astype(jnp.float32))[0]
    grad_bf = grad_pre.astype(jnp.bfloat16)
    out_grad = kernel_grad(padded_s, grad_bf)
    gain_grad = jnp.sum(grad_pre * video.astype(jnp.float32), axis=(0, 1, 2, 3))
    padded_g = pad_columns(padded_2(grad_bf, (("rows", 2),), 1))
    state_grad = adjoint_conv(padded_g, out_kernel)
    local_adjoint = jnp.einsum(
        "tkp,strcp->skrcp", within, state_grad, precision=lax.Precision.HIGHEST
    )
    leading = jnp.exp(cum[0])[None, None, None, :] * local_adjoint[:, 0]
    _, back_in = entering((group_decay, leading), "tm", combine_groups, identity)
    adjoint = (
        local_adjoint
        + jnp.exp(group_total[None, :] - cum)[None, :, None, None, :] * back_in[:, None]
    )
    previous = jnp.concatenate([carry_in[:, None], states[:, :-1]], axis=1)
    decay_part = jnp.sum(
        adjoint * jnp.exp(log_decay)[None, :, None, None, :] * previous, axis=(0, 2, 3)
    )
    decay_scale = 1.0 / math.sqrt(seqs * rows * cols * lax.axis_size("rows") * lax.axis_size("dp"))
    decay_grad = lax.psum(decay_part, ("rows", "dp")) * decay_scale
    adjoint_bf = adjoint.astype(jnp.bfloat16)
    in_grad = kernel_grad(padded_x, adjoint_bf)
    padded_a = pad_columns(padded_2(adjoint_bf, (("rows", 2),), 1))
    video_grad = (adjoint_conv(padded_a, in_kernel) + skip_gain * grad_pre).astype(jnp.bfloat16)
    in_sum, out_sum, gain_sum = lax.psum((in_grad, out_grad, gain_grad), ("tm", "rows", "dp"))
    weight_scale = 1.0 / math.sqrt(
        seqs
        * frames
        * rows
        * cols
        * lax.axis_size("tm")
        * lax.axis_size("rows")
        * lax.axis_size("dp")
    )
    return (
        activated.astype(jnp.bfloat16),
        video_grad,
        in_sum * weight_scale,
        out_sum * weight_scale,
        gain_sum * weight_scale,
        decay_grad,
    )


def solution(mesh):
    placed = (
        P("dp", "tm", "rows", None, None),
        P("dp", "tm", "rows", None, None),
        P(),
        P(),
        P(),
        P("tm", None),
    )
    return jax.shard_map(
        on_device,
        mesh=mesh,
        in_specs=placed,
        out_specs=(
            P("dp", "tm", "rows", None, None),
            P("dp", "tm", "rows", None, None),
            P(),
            P(),
            P(),
            P("tm", None),
        ),
        check_vma=False,
    )
```

profile of v0, /device:TPU:1, one launch (start us, length us, event | category | flops | bytes accessed | tf_op | source)
XLA Modules:
  0.0 644.5 jit_solution(3192037692985163156)
XLA Ops:
  7.2 1.0 fusion.179
  8.2 4.4 collective-permute-start
  12.6 1.3 collective-permute-start.1
  15.3 11.5 %all-gather = f32[8,1,128]{2,1,0:T(1,128)S(1)} all-gather(f32[1,1,128]{2,1,0:T(1,128)S(1)} %get-tuple-element.381), channel_id=1, replica_groups=mesh['tm'=8,'rows'=8,'dp'=4] {'tm'}, dimensions={0}, use_global_device_ids=true | all-gather | bytes 4608 | tf_op jit(solution)/shard_map/all_gather | solution.py:28
  26.9 1.6 fusion.27
  32.4 4.5 copy.179
  36.9 8.3 %fusion.21 = f32[128,4,32,16]{2,3,1,0:T(8,128)} fusion(f32[16,4,32,128]{2,0,1,3:T(8,128)} %copy.179, f32[16,128]{0,1:T(8,128)S(1)} %copy.177, pred[16,16]{0,1:T(8,128)(4,1)S(1)} %iota_compare_fusion.2), kind=kOutput, calls=%fused_computation.80 | convolution fusion | flops 50429952 | bytes 2105600 | tf_op jit(solution)/shard_map/tkp,skrcp->strcp/dot_general | solution.py:127
  45.2 3.7 copy.181
  49.0 13.1 %all_gather.16 = f32[8,1,4,32,128]{4,3,2,1,0:T(8,128)S(1)} all-gather(f32[1,1,4,32,128]{4,3,2,1,0:T(8,128)S(1)} %slice.319), channel_id=1, replica_groups=mesh['tm'=8,'rows'=8,'dp'=4] {'tm'}, dimensions={0}, use_global_device_ids=true | all-gather | bytes 589824 | tf_op jit(solution)/shard_map/all_gather | solution.py:28
  62.6 2.4 fusion.171
  65.0 4.3 collective-permute-start.2
  69.3 1.3 collective-permute-start.3
  70.6 8.7 %all-gather.1 = bf16[8,1,128]{2,1,0:T(2,128)(2,1)S(1)} all-gather(bf16[1,1,128]{2,1,0:T(2,128)(2,1)S(1)} %get-tuple-element.380), channel_id=1, replica_groups=mesh['tm'=8,'rows'=8,'dp'=4] {'tm'}, dimensions={0}, use_global_device_ids=true | all-gather | bytes 2304 | tf_op jit(solution)/shard_map/all_gather | solution.py:43
  79.9 2.3 slice.346
  87.1 2.3 fusion.8
  92.4 1.0 convolution_bitcast_fusion.6
  98.2 4.3 collective-permute-start.4
  102.5 1.3 collective-permute-start.5
  103.8 81.6 %psum.30 = f32[128]{0:T(128)S(1)} all-reduce(f32[128]{0:T(128)S(1)} %copy-done.25), channel_id=1, replica_groups=mesh['tm'=8,'rows'=8,'dp'=4] {'tm','rows','dp'}, use_global_device_ids=true, to_apply=%region_8.9 | all-reduce | flops 128 | bytes 1024 | tf_op jit(solution)/shard_map/psum | solution.py:163
  192.1 4.5 copy.182
  196.6 8.2 %fusion.19 = f32[128,4,32,16]{2,3,1,0:T(8,128)} fusion(f32[16,4,32,128]{2,0,1,3:T(8,128)} %copy.182, f32[16,128]{0,1:T(8,128)S(1)} %copy.177, pred[16,16]{0,1:T(8,128)(4,1)S(1)} %copy-done.21), kind=kOutput, calls=%fused_computation.78 | convolution fusion | flops 50429952 | bytes 2105600 | tf_op jit(solution)/shard_map/tkp,strcp->skrcp/dot_general | solution.py:144
  204.8 3.7 copy.183
  208.5 13.5 %all_gather.18 = bf16[8,1,4,32,128]{4,3,2,1,0:T(8,128)(2,1)S(1)} all-gather(bf16[1,1,4,32,128]{4,3,2,1,0:T(8,128)(2,1)S(1)} %fusion.73), channel_id=1, replica_groups=mesh['tm'=8,'rows'=8,'dp'=4] {'tm'}, dimensions={0}, use_global_device_ids=true | all-gather | bytes 294912 | tf_op jit(solution)/shard_map/all_gather | solution.py:43
  222.1 5.9 while.31
  228.0 1.5 fusion.18
  233.0 3.4 collective-permute-start.6
  236.5 1.3 collective-permute-start.7
  237.9 114.3 %psum.31 = f32[16,128]{0,1:T(8,128)S(1)} all-reduce(f32[16,128]{0,1:T(8,128)S(1)} %copy.211), channel_id=1, replica_groups=mesh['tm'=8,'rows'=8,'dp'=4] {'rows','dp'}, use_global_device_ids=true, to_apply=%region_10.11 | all-reduce | flops 2048 | bytes 16384 | tf_op jit(solution)/shard_map/psum | solution.py:158
  358.9 1.0 add_convert_fusion
  359.9 273.7 %all-reduce.7.cloned.1.call-done = (f32[3,3,128,128]{3,2,1,0:T(8,128)}, f32[3,3,128,128]{3,2,1,0:T(8,128)}) async-done(((f32[3,3,128,128]{3,2,1,0:T(8,128)}, f32[3,3,128,128]{3,2,1,0:T(8,128)}), (f32[3,3,128,128]{3,2,1,0:T(8,128)}, f32[3,3,128,128]{3,2,1,0:T(8,128)})) %all-reduce.7.cloned.1.call-update) | async-done | bytes 1179664 | tf_op jit(solution)/shard_map/psum | solution.py:163
  633.6 1.9 broadcast_multiply_fusion
  635.5 1.9 broadcast_multiply_fusion.1
  (182 shorter events, 41.7 us)
Async XLA Ops:
  7.2 626.5 %all-reduce.7.cloned.1.call-start = ((), (), s32[]{:S(2)}) async-start(), calls=%async_computation | async-start | bytes 2359296 | tf_op jit(solution)/shard_map/psum | solution.py:163
  8.2 18.6 %collective-permute-start = (bf16[1,16,1,32,128]{4,3,2,1,0:T(8,128)(2,1)S(1)}, bf16[1,16,1,32,128]{4,3,2,1,0:T(8,128)(2,1)S(1)}, u32[]{:S(2)}, u32[]{:S(2)}) collective-permute-start(bf16[1,16,1,32,128]{4,3,2,1,0:T(8,128)(2,1)S(1)} %get-tuple-element.375), channel_id=1, source_target_pairs={{0,4},{4,8},{8,12},{12,16},{16,20},{20,24},{24,28},{1,5},{5,9},{9,... | collective-permute-start | bytes 393224 | tf_op jit(solution)/shard_map/ppermute | solution.py:17
  12.6 14.3 %collective-permute-start.1 = (bf16[1,16,1,32,128]{4,3,2,1,0:T(8,128)(2,1)S(1)}, bf16[1,16,1,32,128]{4,3,2,1,0:T(8,128)(2,1)S(1)}, u32[]{:S(2)}, u32[]{:S(2)}) collective-permute-start(bf16[1,16,1,32,128]{4,3,2,1,0:T(8,128)(2,1)S(1)} %get-tuple-element.376), channel_id=1, source_target_pairs={{4,0},{8,4},{12,8},{16,12},{20,16},{24,20},{28,24},{5,1},{9,5},{13... | collective-permute-start | bytes 393224 | tf_op jit(solution)/shard_map/ppermute | solution.py:19
  26.8 10.1 %copy-start.20 = (pred[16,16]{0,1:T(8,128)(4,1)}, pred[16,16]{0,1:T(8,128)(4,1)S(1)}, u32[]{:S(2)}) copy-start(pred[16,16]{0,1:T(8,128)(4,1)S(1)} %iota_compare_fusion.2) | copy-start | bytes 772
  28.5 1.0 copy-start.10
  29.1 1.1 copy-start
  30.2 1.9 copy-start.4
  49.0 13.6 %copy-start.3 = (f32[128,4,32,16]{0,2,1,3:T(8,128)}, f32[128,4,32,16]{0,2,1,3:T(8,128)S(1)}, u32[]{:S(2)}) copy-start(f32[128,4,32,16]{0,2,1,3:T(8,128)S(1)} %copy.181) | copy-start | bytes 3145732
  62.1 8.5 %copy-start.19 = (f32[16,128]{1,0:T(8,128)S(1)}, f32[16,128]{1,0:T(8,128)}, u32[]{:S(2)}) copy-start(f32[16,128]{1,0:T(8,128)} %param.15) | copy-start | bytes 24580
  65.0 17.2 %collective-permute-start.2 = (bf16[1,16,1,32,128]{4,3,2,1,0:T(8,128)(2,1)S(1)}, bf16[1,16,1,32,128]{4,3,2,1,0:T(8,128)(2,1)S(1)}, u32[]{:S(2)}, u32[]{:S(2)}) collective-permute-start(bf16[1,16,1,32,128]{4,3,2,1,0:T(8,128)(2,1)S(1)} %get-tuple-element.371), channel_id=1, source_target_pairs={{0,4},{4,8},{8,12},{12,16},{16,20},{20,24},{24,28},{1,5},{5,9},{9,... | collective-permute-start | bytes 393224 | tf_op jit(solution)/shard_map/ppermute | solution.py:17
  69.3 12.9 %collective-permute-start.3 = (bf16[1,16,1,32,128]{4,3,2,1,0:T(8,128)(2,1)S(1)}, bf16[1,16,1,32,128]{4,3,2,1,0:T(8,128)(2,1)S(1)}, u32[]{:S(2)}, u32[]{:S(2)}) collective-permute-start(bf16[1,16,1,32,128]{4,3,2,1,0:T(8,128)(2,1)S(1)} %get-tuple-element.372), channel_id=1, source_target_pairs={{4,0},{8,4},{12,8},{16,12},{20,16},{24,20},{28,24},{5,1},{9,5},{13... | collective-permute-start | bytes 393224 | tf_op jit(solution)/shard_map/ppermute | solution.py:19
  82.7 1.0 copy-start.8
  86.0 1.0 copy-start.12
  86.0 1.0 copy-start.23
  89.4 2.0 copy-start.1
  96.2 7.6 %copy-start.25 = (f32[128]{0:T(128)S(1)}, f32[128]{0:T(128)}, u32[]{:S(2)}) copy-start(f32[128]{0:T(128)} %get-tuple-element.330) | copy-start | bytes 1540
  96.2 89.8 %copy-start.13 = (f32[1,128,128]{2,1,0:T(8,128)S(1)}, f32[1,128,128]{2,1,0:T(8,128)}, u32[]{:S(2)}) copy-start(f32[1,128,128]{2,1,0:T(8,128)} %convolution_bitcast_fusion.7) | copy-start | bytes 196612
  96.2 89.8 %copy-start.14 = (f32[1,128,128]{2,1,0:T(8,128)S(1)}, f32[1,128,128]{2,1,0:T(8,128)}, u32[]{:S(2)}) copy-start(f32[1,128,128]{2,1,0:T(8,128)} %convolution_bitcast_fusion.3) | copy-start | bytes 196612
  96.2 89.8 %copy-start.15 = (f32[1,128,128]{2,1,0:T(8,128)S(1)}, f32[1,128,128]{2,1,0:T(8,128)}, u32[]{:S(2)}) copy-start(f32[1,128,128]{2,1,0:T(8,128)} %convolution_bitcast_fusion.5) | copy-start | bytes 196612
  96.3 89.8 %copy-start.16 = (f32[1,128,128]{2,1,0:T(8,128)S(1)}, f32[1,128,128]{2,1,0:T(8,128)}, u32[]{:S(2)}) copy-start(f32[1,128,128]{2,1,0:T(8,128)} %convolution_bitcast_fusion.6) | copy-start | bytes 196612
  96.3 89.7 %copy-start.17 = (f32[1,128,128]{2,1,0:T(8,128)S(1)}, f32[1,128,128]{2,1,0:T(8,128)}, u32[]{:S(2)}) copy-start(f32[1,128,128]{2,1,0:T(8,128)} %convolution_bitcast_fusion.8) | copy-start | bytes 196612
  96.3 89.7 %copy-start.18 = (f32[1,128,128]{2,1,0:T(8,128)S(1)}, f32[1,128,128]{2,1,0:T(8,128)}, u32[]{:S(2)}) copy-start(f32[1,128,128]{2,1,0:T(8,128)} %convolution_bitcast_fusion.4) | copy-start | bytes 196612
  98.2 89.6 %collective-permute-start.4 = (bf16[1,16,1,32,128]{4,3,2,1,0:T(8,128)(2,1)S(1)}, bf16[1,16,1,32,128]{4,3,2,1,0:T(8,128)(2,1)S(1)}, u32[]{:S(2)}, u32[]{:S(2)}) collective-permute-start(bf16[1,16,1,32,128]{4,3,2,1,0:T(8,128)(2,1)S(1)} %get-tuple-element.367), channel_id=1, source_target_pairs={{0,4},{4,8},{8,12},{12,16},{16,20},{20,24},{24,28},{1,5},{5,9},{9,... | collective-permute-start | bytes 393224 | tf_op jit(solution)/shard_map/ppermute | solution.py:17
  102.5 85.3 %collective-permute-start.5 = (bf16[1,16,1,32,128]{4,3,2,1,0:T(8,128)(2,1)S(1)}, bf16[1,16,1,32,128]{4,3,2,1,0:T(8,128)(2,1)S(1)}, u32[]{:S(2)}, u32[]{:S(2)}) collective-permute-start(bf16[1,16,1,32,128]{4,3,2,1,0:T(8,128)(2,1)S(1)} %get-tuple-element.368), channel_id=1, source_target_pairs={{4,0},{8,4},{12,8},{16,12},{20,16},{24,20},{28,24},{5,1},{9,5},{13... | collective-permute-start | bytes 393224 | tf_op jit(solution)/shard_map/ppermute | solution.py:19
  192.1 4.5 copy-start.21
  204.8 3.7 copy-start.22
  229.8 1.0 copy-start.5
  230.2 1.1 copy-start.7
  233.0 120.7 %collective-permute-start.6 = (bf16[1,16,1,32,128]{4,3,2,1,0:T(8,128)(2,1)S(1)}, bf16[1,16,1,32,128]{4,3,2,1,0:T(8,128)(2,1)S(1)}, u32[]{:S(2)}, u32[]{:S(2)}) collective-permute-start(bf16[1,16,1,32,128]{4,3,2,1,0:T(8,128)(2,1)S(1)} %get-tuple-element.363), channel_id=1, source_target_pairs={{0,4},{4,8},{8,12},{12,16},{16,20},{20,24},{24,28},{1,5},{5,9},{9,... | collective-permute-start | bytes 393224 | tf_op jit(solution)/shard_map/ppermute | solution.py:17
  236.5 117.3 %collective-permute-start.7 = (bf16[1,16,1,32,128]{4,3,2,1,0:T(8,128)(2,1)S(1)}, bf16[1,16,1,32,128]{4,3,2,1,0:T(8,128)(2,1)S(1)}, u32[]{:S(2)}, u32[]{:S(2)}) collective-permute-start(bf16[1,16,1,32,128]{4,3,2,1,0:T(8,128)(2,1)S(1)} %get-tuple-element.364), channel_id=1, source_target_pairs={{4,0},{8,4},{12,8},{16,12},{20,16},{24,20},{28,24},{5,1},{9,5},{13... | collective-permute-start | bytes 393224 | tf_op jit(solution)/shard_map/ppermute | solution.py:19
  357.7 1.2 copy-start.2
  357.7 1.2 copy-start.24
  (3 other events, 2.7 us)
Sparse Core Ops, SparseCore 0:
  353.8 279.7 all-reduce.6
where the time goes:
time: 655 us; the launch traced here: 645 us
  waiting for transfers between devices  274 us (42%)
  blocking collectives  243 us (37%)
  matrix products  38.6 us (6%)
  local copies, waits for them, and re-layouts  27.4 us (4%)
  other arithmetic  25 us (4%)
  starting transfers between devices  21.6 us (3%)
  between operations  15 us (2%)
    psum x1, waiting for transfers between devices, on_device(): lax.psum((in_grad, out_grad, gain_grad), ('tm', 'rows', 'dp'))  274 us
    psum x1, blocking collectives, on_device(): decay_grad = lax.psum(decay_part, ('rows', 'dp')) * decay_scale  114 us
    psum x1, blocking collectives, on_device(): lax.psum((in_grad, out_grad, gain_grad), ('tm', 'rows', 'dp'))  81.6 us
    all_gather x2, blocking collectives, prefix(): pieces = jax.tree.map(lambda part: lax.all_gather(part, axis), value)  24.6 us
    all_gather x2, blocking collectives, entering(): lax.all_gather(part.astype(kind), axis)  22.3 us
    ppermute x4, starting transfers between devices, padded_2(): lax.ppermute(tail, axis, [(i, (i + 1) % count) for i in range(ends)])  16.4 us
  transfers between devices with their start and end apart: 9, of which 1 were waited for; matrix products, arithmetic and copies ran while one was open for 2% of the time, Pallas kernels for 0%

commit v1 on v0

v1 whole, which is shorter than its diff:
```python
import functools
import math

import jax
import jax.numpy as jnp
from jax import lax
from jax.experimental import pallas as pl
from jax.experimental.pallas import tpu as pltpu
from jax.sharding import PartitionSpec as P

MESH = pl.DeviceIdType.MESH
F32, BF16 = jnp.float32, jnp.bfloat16
C = 128
TAPS = 3
LANES = TAPS * C
GELU_A = math.sqrt(2.0 / math.pi)
GELU_B = 0.044715


def at_next(field):
    cols = field.shape[1]
    col = lax.broadcasted_iota(jnp.int32, field.shape, 1)
    return jnp.where(col == cols - 1, 0.0, pltpu.roll(field, cols - 1, 1))


def at_previous(field):
    col = lax.broadcasted_iota(jnp.int32, field.shape, 1)
    return jnp.where(col == 0, 0.0, pltpu.roll(field, 1, 1))


def taps(w_ref, i):
    return jnp.concatenate([w_ref[i, j] for j in range(TAPS)], axis=-1)


def forward_rows(pad, w_ref, frames, r0, nr):
    n, cols = frames.size * nr, pad.shape[2]
    lhs = jnp.concatenate(
        [pad[frames, r0 + i : r0 + i + nr].reshape(n * cols, C) for i in range(TAPS)], axis=-1
    )
    rhs = jnp.concatenate([taps(w_ref, i) for i in range(TAPS)], axis=0)
    y = jnp.dot(lhs, rhs, preferred_element_type=F32).reshape(n, cols, LANES)
    return at_previous(y[..., :C]) + y[..., C : 2 * C] + at_next(y[..., 2 * C :])


def adjoint_rows(wide, w_ref, frames, r0, nr):
    n, cols = frames.size * nr, wide.shape[2]
    lhs = jnp.concatenate(
        [wide[frames, r0 + 2 - i : r0 + 2 - i + nr].reshape(n * cols, LANES) for i in range(TAPS)],
        axis=-1,
    )
    rhs = jnp.concatenate([taps(w_ref, i) for i in range(TAPS)], axis=-1)
    y = lax.dot_general(lhs, rhs, (((1,), (1,)), ((), ())), preferred_element_type=F32)
    return y.reshape(n, cols, C)


def widen(wide, frames, r0, nr, value):
    shape = (frames.size, nr) + value.shape[1:]
    for j, part in enumerate((at_next(value), value, at_previous(value))):
        wide[frames, r0 : r0 + nr, :, j * C : (j + 1) * C] = part.astype(BF16).reshape(shape)


def body(
    nt, nz, nx, total_cells, total_positions,
    x_hbm, ct_hbm, w_in, w_out, gain, ld,
    lo_hbm, vg_hbm, ig_out, og_out, gg_out, dg_out,
    xpad, spad, g3, a3, st, ag, gp, ct, lo, vg,
    es, eg, ea, hs, hg, ha, ces, cer,
    lam, ecum, erev, dsend, dall, csend, crecv, cin, bin_, gsum, dpart,
    acc, snd1, rcv1, snd2, rcv2, x3, f4, g5,
    loc, hal_s, hal_r, ce_s, ce_r, dec_s, dec_r, car_s, car_r,
    p1_s, p1_r, p2_s, p2_r, p3_s, p3_r, p4_s, p4_r, p5_s, p5_r,
):
    T, R, W, _ = x_hbm.shape
    CH = LANES // nt
    SR = TAPS * CH + 16
    BR = snd2.shape[1] // (-(-SR // rcv2.shape[2]))
    NB = snd2.shape[1] // BR
    half = T // 2
    all_frames = pl.ds(0, T)
    me, mez, mex = lax.axis_index("tm"), lax.axis_index("rows"), lax.axis_index("dp")

    def to_tm(src, dst, s, r, k):
        return pltpu.make_async_remote_copy(src, dst, s, r, device_id={"tm": k}, device_id_type=MESH)

    def to_rows(src, dst, s, r, k):
        return pltpu.make_async_remote_copy(src, dst, s, r, device_id={"rows": k}, device_id_type=MESH)

    def to_dp(src, dst, s, r, k):
        return pltpu.make_async_remote_copy(src, dst, s, r, device_id={"dp": k}, device_id_type=MESH)

    def others(mine, count, act):
        def step(o, _):
            act(lax.rem(mine + o, count))
            return 0

        lax.fori_loop(1, count, step, 0)

    def each(low, high, act):
        def step(k, _):
            act(k)
            return 0

        lax.fori_loop(low, high, step, 0)

    barrier = pltpu.get_barrier_semaphore()
    for axis, mine, count in (("tm", me, nt), ("rows", mez, nz), ("dp", mex, nx)):
        others(
            mine, count,
            lambda k, axis=axis: pl.semaphore_signal(
                barrier, inc=1, device_id={axis: k}, device_id_type=MESH
            ),
        )
    load_x = pltpu.make_async_copy(x_hbm, xpad.at[:, 1 : R + 1], loc.at[0])
    load_x.start()
    load_ct = pltpu.make_async_copy(ct_hbm, ct, loc.at[1])
    load_ct.start()

    run = jnp.zeros((1, C), F32)
    for t in range(T):
        run = run + ld[t : t + 1]
        ecum[t : t + 1] = run
    erev[...] = jnp.exp(run - ecum[...])
    ecum[...] = jnp.exp(ecum[...])
    lam[...] = jnp.exp(ld[...])
    dsend[...] = jnp.broadcast_to(jnp.exp(run), dsend.shape)
    gsum[...] = jnp.zeros_like(gsum)

    @pl.when(mez == 0)
    def _():
        for ref in (xpad, spad, g3, a3):
            ref[:, 0] = jnp.zeros((T, W, ref.shape[3]), BF16)

    @pl.when(mez == nz - 1)
    def _():
        for ref in (xpad, spad, g3, a3):
            ref[:, R + 1] = jnp.zeros((T, W, ref.shape[3]), BF16)

    pl.semaphore_wait(barrier, nt + nz + nx - 3)

    def edge(stage, way, src, dst, sems=None):
        s, r = sems or (hal_s, hal_r)
        return to_rows(
            src, dst, s.at[stage, way], r.at[stage, way],
            jnp.maximum(mez - 1, 0) if way == 0 else jnp.minimum(mez + 1, nz - 1),
        )

    def edges(stage, srcs, dsts, what, sems=None):
        for way in range(2):
            from_there = (mez < nz - 1) if way == 0 else (mez > 0)
            to_there = (mez > 0) if way == 0 else (mez < nz - 1)

            @pl.when(from_there if what == "recv" else to_there)
            def _(way=way):
                copy = edge(stage, way, srcs[way], dsts[way], sems)
                {"start": copy.start, "recv": copy.wait_recv, "send": copy.wait_send}[what]()

    def received(act):
        @pl.when(mez < nz - 1)
        def _():
            act(0, R + 1)

        @pl.when(mez > 0)
        def _():
            act(1, 0)

    edge_sets = [
        (0, (x_hbm.at[:, 0], x_hbm.at[:, R - 1]), (xpad.at[:, R + 1], xpad.at[:, 0]), None),
        (1, (es.at[0], es.at[1]), (hs.at[0], hs.at[1]), None),
        (2, (eg.at[0], eg.at[1]), (hg.at[0], hg.at[1]), None),
        (3, (ea.at[0], ea.at[1]), (ha.at[0], ha.at[1]), None),
        (0, (ces.at[0, 0], ces.at[0, 1]), (cer.at[0, 0], cer.at[0, 1]), (ce_s, ce_r)),
        (1, (ces.at[1, 0], ces.at[1, 1]), (cer.at[1, 0], cer.at[1, 1]), (ce_s, ce_r)),
    ]

    def do_edges(n, what):
        stage, srcs, dsts, sems = edge_sets[n]
        edges(stage, srcs, dsts, what, sems)

    do_edges(0, "start")

    def decay_copy(k):
        return to_tm(dsend, dall.at[me], dec_s.at[k], dec_r.at[me], k)

    others(me, nt, lambda k: decay_copy(k).start())

    def send1(q, k):
        return to_tm(snd1.at[q, k], rcv1.at[q, me], p1_s.at[q, k], p1_r.at[q, me], k)

    def send2(q, k):
        return to_rows(
            snd2.at[q, pl.ds(k * BR, BR)], rcv2.at[q, mez], p2_s.at[q, k], p2_r.at[q, mez], k
        )

    def send3(q, k):
        return to_dp(x3.at[q, mex], x3.at[q, mex], p3_s.at[q, k], p3_r.at[q, mex], k)

    def send4(q, k):
        here = f4.at[q, pl.ds(mez * BR, BR)]
        return to_rows(here, here, p4_s.at[q, k], p4_r.at[q, mez], k)

    def send5(q, k):
        return to_tm(f4.at[q], g5.at[q, me], p5_s.at[q, k], p5_r.at[q, me], k)

    def got(ref, q, k, r, copy):
        return copy(ref.at[q, k], ref.at[q, k], r.at[q, k], r.at[q, k], 0).wait_recv()

    def not_me(k, act):
        @pl.when(k != mez)
        def _():
            act(k)

    def sum1(q):
        for k in range(nt):
            snd1[q, k] = acc[q, k * CH : (k + 1) * CH].astype(BF16)
        others(me, nt, lambda k: send1(q, k).start())

    def sum2(q, extra):
        def step(o, total):
            k = lax.rem(me + o, nt)
            got(rcv1, q, k, p1_r, to_tm)
            return total + rcv1[q, k].astype(F32)

        total = lax.fori_loop(1, nt, step, acc[q, pl.ds(pl.multiple_of(me * CH, 16), CH)])
        for j in range(TAPS):
            snd2[q, j * CH : (j + 1) * CH] = total[:, j * C : (j + 1) * C].astype(BF16)
        snd2[q, TAPS * CH : SR] = extra.astype(BF16)
        if NB * BR > SR:
            snd2[q, SR:] = jnp.zeros((NB * BR - SR, C), BF16)
        each(0, NB, lambda k: not_me(k, lambda k: send2(q, k).start()))

    def sum3(q):
        @pl.when(mez < NB)
        def _():
            def step(o, total):
                k = lax.rem(mez + o, nz)
                got(rcv2, q, k, p2_r, to_rows)
                return total + rcv2[q, k].astype(F32)

            mine = snd2[q, pl.ds(pl.multiple_of(mez * BR, 16), BR)].astype(F32)
            x3[q, mex] = lax.fori_loop(1, nz, step, mine)
            others(mex, nx, lambda k: send3(q, k).start())

    def sum4(q):
        @pl.when(mez < NB)
        def _():
            others(mex, nx, lambda k: got(x3, q, k, p3_r, to_dp))
            total = x3[q, 0]
            for k in range(1, nx):
                total = total + x3[q, k]
            f4[q, pl.ds(pl.multiple_of(mez * BR, 16), BR)] = total.astype(BF16)
            others(mez, nz, lambda k: send4(q, k).start())

    def sum5(q):
        def wait(k):
            there = f4.at[q, pl.ds(k * BR, BR)]
            to_rows(there, there, p4_s.at[q, k], p4_r.at[q, k], 0).wait_recv()

        each(0, NB, lambda k: not_me(k, wait))
        g5[q, me] = f4[q]
        others(me, nt, lambda k: send5(q, k).start())

    weight_scale = 1.0 / math.sqrt(total_positions)

    def sum6(q, out):
        others(me, nt, lambda k: got(g5, q, k, p5_r, to_tm))
        for k in range(nt):
            for u in range(0, CH, 16):
                i, c = divmod(k * CH + u, C)
                for j in range(TAPS):
                    piece = g5[q, k, j * CH + u : j * CH + u + 16]
                    out[i, j, c : c + 16] = piece.astype(F32) * weight_scale

    def sums_sent(q):
        others(me, nt, lambda k: send1(q, k).wait_send())
        each(0, NB, lambda k: not_me(k, lambda k: send2(q, k).wait_send()))

        @pl.when(mez < NB)
        def _():
            others(mex, nx, lambda k: send3(q, k).wait_send())
            others(mez, nz, lambda k: send4(q, k).wait_send())

        others(me, nt, lambda k: send5(q, k).wait_send())

    def inner(act):
        each(0, 2, lambda f: act(pl.ds(f * half, half), 1, R - 2))

    def outer(act):
        each(0, 1, lambda f: act(all_frames, 0, 1))
        each(0, 1, lambda f: act(all_frames, R - 1, 1))

    def drive(frames, r0, nr):
        y = forward_rows(xpad, w_in, frames, r0, nr)
        ag[frames, r0 : r0 + nr] = y.reshape(frames.size, nr, W, C)

    load_x.wait()
    inner(drive)
    do_edges(0, "recv")
    outer(drive)

    def forward_step(t, state):
        state = lam[pl.ds(t, 1)].reshape(1, 1, C) * state + ag[t]
        st[t + 1] = state
        es[0, t] = state[0].astype(BF16)
        es[1, t] = state[R - 1].astype(BF16)
        return state

    last = lax.fori_loop(0, T, forward_step, jnp.zeros((R, W, C), F32))
    csend[0] = last.astype(BF16)

    def carry_copy(way, k):
        return to_tm(csend.at[way], crecv.at[way, me], car_s.at[way, k], car_r.at[way, me], k)

    each(me + 1, nt, lambda k: carry_copy(0, k).start())
    do_edges(1, "start")

    others(me, nt, lambda k: to_tm(dsend, dall.at[k], dec_s.at[k], dec_r.at[k], 0).wait_recv())

    def join_earlier(k, state):
        got(crecv, 0, k, car_r, to_tm)
        return dall[k, 0:1].reshape(1, 1, C) * state + crecv[0, k].astype(F32)

    carry = lax.fori_loop(0, me, join_earlier, jnp.zeros((R, W, C), F32))
    ces[0, 0] = carry[0].astype(BF16)
    ces[0, 1] = carry[R - 1].astype(BF16)
    do_edges(4, "start")
    st[0] = carry
    cin[...] = carry

    def finish_state(t):
        state = st[t + 1] + ecum[pl.ds(t, 1)].reshape(1, 1, C) * cin[...]
        st[t + 1] = state
        spad[t, 1 : R + 1] = state.astype(BF16)

    each(0, T, finish_state)

    load_ct.wait()

    def output(frames, r0, nr):
        n = frames.size * nr
        x = xpad[frames, r0 + 1 : r0 + 1 + nr].reshape(n, W, C).astype(F32)
        pre = forward_rows(spad, w_out, frames, r0, nr) + gain[...].reshape(1, 1, C) * x
        square = pre * pre
        bend = jnp.tanh(GELU_A * (pre + GELU_B * (square * pre)))
        rise = 0.5 * (1.0 + bend)
        lo[frames, r0 : r0 + nr] = (pre * rise).astype(BF16).reshape(frames.size, nr, W, C)
        slope = rise + 0.5 * pre * (1.0 - bend * bend) * (GELU_A * (1.0 + 3.0 * GELU_B * square))
        grad = ct[frames, r0 : r0 + nr].reshape(n, W, C).astype(F32) * slope
        gp[frames, r0 : r0 + nr] = grad.reshape(frames.size, nr, W, C)
        gsum[...] += jnp.sum((grad * x).reshape(n * W // 8, 8, C), axis=0)
        widen(g3, frames, r0 + 1, nr, grad)

    inner(output)
    do_edges(1, "recv")
    do_edges(4, "recv")

    def state_edge(way, row):
        def step(t):
            value = hs[way, t].astype(F32) + ecum[pl.ds(t, 1)] * cer[0, way].astype(F32)
            spad[t, row] = value.astype(BF16)

        each(0, T, step)

    received(state_edge)
    outer(output)
    eg[0] = gp[:, 0].astype(BF16)
    eg[1] = gp[:, R - 1].astype(BF16)
    do_edges(2, "start")
    store_lo = pltpu.make_async_copy(lo, lo_hbm, loc.at[2])
    store_lo.start()

    def kernel_grad(q, pad, wide):
        acc[q] = jnp.zeros((LANES, LANES), F32)
        part = T // 4

        def step(f):
            frames = pl.ds(f * part, part)
            n = part * R * W
            lhs = jnp.concatenate(
                [pad[frames, i : i + R].reshape(n, C) for i in range(TAPS)], axis=-1
            )
            rhs = wide[frames, 1 : R + 1].reshape(n, LANES)
            acc[q] += lax.dot_general(
                lhs, rhs, (((0,), (0,)), ((), ())), preferred_element_type=F32
            )

        each(0, 4, step)

    kernel_grad(0, spad, g3)
    sum1(0)

    def state_grad(frames, r0, nr):
        ag[frames, r0 : r0 + nr] = adjoint_rows(g3, w_out, frames, r0, nr).reshape(
            frames.size, nr, W, C
        )

    inner(state_grad)
    do_edges(2, "recv")
    received(lambda way, row: widen(g3, all_frames, row, 1, hg[way].astype(F32)))
    outer(state_grad)

    def backward_step(o, carried):
        t = T - 1 - o
        adjoint = ag[t] + carried
        ag[t] = adjoint
        ea[0, t] = adjoint[0].astype(BF16)
        ea[1, t] = adjoint[R - 1].astype(BF16)
        return lam[pl.ds(t, 1)].reshape(1, 1, C) * adjoint

    first = lax.fori_loop(0, T, backward_step, jnp.zeros((R, W, C), F32))
    csend[1] = first.astype(BF16)
    each(0, me, lambda k: carry_copy(1, k).start())
    do_edges(3, "start")

    zeros8 = jnp.zeros((8, C), F32)
    sum2(0, jnp.concatenate([gsum[...], zeros8], axis=0))

    def join_later(o, adjoint):
        k = nt - 1 - o
        got(crecv, 1, k, car_r, to_tm)
        return dall[k, 0:1].reshape(1, 1, C) * adjoint + crecv[1, k].astype(F32)

    back = lax.fori_loop(0, nt - 1 - me, join_later, jnp.zeros((R, W, C), F32))
    ces[1, 0] = back[0].astype(BF16)
    ces[1, 1] = back[R - 1].astype(BF16)
    do_edges(5, "start")
    bin_[...] = back

    def finish_adjoint(t):
        adjoint = ag[t] + erev[pl.ds(t, 1)].reshape(1, 1, C) * bin_[...]
        product = jnp.sum((adjoint * st[t]).reshape(R * W, C), axis=0, keepdims=True)
        dpart[pl.ds(t, 1)] = product * lam[pl.ds(t, 1)]
        for j, part in enumerate((at_next(adjoint), adjoint, at_previous(adjoint))):
            a3[t, 1 : R + 1, :, j * C : (j + 1) * C] = part.astype(BF16)

    each(0, T, finish_adjoint)
    kernel_grad(1, xpad, a3)
    sum1(1)
    sum3(0)

    def video_grad(frames, r0, nr):
        skip = gain[...].reshape(1, 1, C) * gp[frames, r0 : r0 + nr].reshape(-1, W, C)
        value = adjoint_rows(a3, w_in, frames, r0, nr) + skip
        vg[frames, r0 : r0 + nr] = value.astype(BF16).reshape(frames.size, nr, W, C)

    inner(video_grad)
    sum2(1, dpart[...])
    sum4(0)
    do_edges(3, "recv")
    do_edges(5, "recv")

    def adjoint_edge(way, row):
        def step(t):
            value = ha[way, t].astype(F32) + erev[pl.ds(t, 1)] * cer[1, way].astype(F32)
            widen(a3, pl.ds(t, 1), row, 1, value.reshape(1, W, C))

        each(0, T, step)

    received(adjoint_edge)
    sum3(1)
    sum5(0)
    outer(video_grad)
    store_vg = pltpu.make_async_copy(vg, vg_hbm, loc.at[3])
    store_vg.start()
    sum4(1)
    sum6(0, og_out)
    sum5(1)
    dg_out[...] = f4[1, TAPS * CH : SR].astype(F32) * (1.0 / math.sqrt(total_cells))
    total_gain = jnp.zeros((8, C), F32)
    for k in range(nt):
        total_gain = total_gain + g5[0, k, TAPS * CH : SR].astype(F32)[0:8]
    gg_out[...] = jnp.sum(total_gain, axis=0, keepdims=True) * weight_scale
    sum6(1, ig_out)

    for n in range(6):
        do_edges(n, "send")
    others(me, nt, lambda k: decay_copy(k).wait_send())
    each(me + 1, nt, lambda k: carry_copy(0, k).wait_send())
    each(0, me, lambda k: carry_copy(1, k).wait_send())
    for q in range(2):
        sums_sent(q)
    store_lo.wait()
    store_vg.wait()


def on_device(nt, nz, nx, video, cotangent, in_kernel, out_kernel, skip_gain, log_decay):
    seqs, T, R, W, _ = video.shape
    field = (T, R, W, C)
    CH = LANES // nt
    SR = TAPS * CH + 16
    BR = -(-SR // (nz * 16)) * 16
    NB = -(-SR // BR)
    dma = pltpu.SemaphoreType.DMA
    vmem = pltpu.VMEM
    scratch = [
        vmem((T, R + 2, W, C), BF16),
        vmem((T, R + 2, W, C), BF16),
        vmem((T, R + 2, W, LANES), BF16),
        vmem((T, R + 2, W, LANES), BF16),
        vmem((T + 1, R, W, C), F32),
        vmem(field, F32),
        vmem(field, F32),
        vmem(field, BF16),
        vmem(field, BF16),
        vmem(field, BF16),
        *[vmem((2, T, W, C), BF16)] * 6,
        *[vmem((2, 2, W, C), BF16)] * 2,
        *[vmem((T, C), F32)] * 3,
        vmem((8, C), F32),
        vmem((nt, 8, C), F32),
        vmem((2, R, W, C), BF16),
        vmem((2, nt, R, W, C), BF16),
        vmem((R, W, C), F32),
        vmem((R, W, C), F32),
        vmem((8, C), F32),
        vmem((T, C), F32),
        vmem((2, LANES, LANES), F32),
        vmem((2, nt, CH, LANES), BF16),
        vmem((2, nt, CH, LANES), BF16),
        vmem((2, NB * BR, C), BF16),
        vmem((2, nz, BR, C), BF16),
        vmem((2, nx, BR, C), F32),
        vmem((2, NB * BR, C), BF16),
        vmem((2, nt, NB * BR, C), BF16),
        dma((4,)),
        dma((4, 2)),
        dma((4, 2)),
        dma((2, 2)),
        dma((2, 2)),
        dma((nt,)),
        dma((nt,)),
        *[dma((2, nt))] * 4,
        *[dma((2, nz))] * 2,
        *[dma((2, nx))] * 2,
        *[dma((2, nz))] * 2,
        *[dma((2, nt))] * 2,
    ]
    any_, whole = pl.BlockSpec(memory_space=pl.ANY), pl.BlockSpec(memory_space=pltpu.VMEM)
    cells = seqs * nx * R * nz * W
    outs = pl.pallas_call(
        functools.partial(body, nt, nz, nx, cells, cells * T * nt),
        out_shape=(
            jax.ShapeDtypeStruct(field, BF16),
            jax.ShapeDtypeStruct(field, BF16),
            jax.ShapeDtypeStruct((TAPS, TAPS, C, C), F32),
            jax.ShapeDtypeStruct((TAPS, TAPS, C, C), F32),
            jax.ShapeDtypeStruct((1, C), F32),
            jax.ShapeDtypeStruct((T, C), F32),
        ),
        in_specs=[any_, any_, whole, whole, whole, whole],
        out_specs=(any_, any_, whole, whole, whole, whole),
        scratch_shapes=scratch,
        compiler_params=pltpu.CompilerParams(
            collective_id=0, has_side_effects=True, vmem_limit_bytes=48 * 2**20
        ),
    )(
        video.reshape(field),
        cotangent.reshape(field),
        in_kernel,
        out_kernel,
        skip_gain.reshape(1, C),
        log_decay,
    )
    layer_out, video_grad, in_grad, out_grad, gain_grad, decay_grad = outs
    return (
        layer_out.reshape(video.shape),
        video_grad.reshape(video.shape),
        in_grad,
        out_grad,
        gain_grad.reshape(C),
        decay_grad,
    )


def solution(mesh):
    field = P("dp", "tm", "rows", None, None)
    nt, nz, nx = mesh.shape["tm"], mesh.shape["rows"], mesh.shape["dp"]
    return jax.shard_map(
        functools.partial(on_device, nt, nz, nx),
        mesh=mesh,
        in_specs=(field, field, P(), P(), P(), P("tm", None)),
        out_specs=(field, field, P(), P(), P(), P("tm", None)),
        check_vma=False,
    )
```

time: 655 us -> 73.9 us (0.11); the launches traced: 645 us -> 73.6 us
  waiting for transfers between devices: 274 us -> 0 us
  blocking collectives: 243 us -> 0 us
  Pallas kernels: 0 us -> 63.3 us
  matrix products: 38.6 us -> 0 us
  other arithmetic: 25 us -> 0 us
  starting transfers between devices: 21.6 us -> 0 us
  local copies, waits for them, and re-layouts: 27.4 us -> 9.67 us
  between operations: 15 us -> 0.66 us
    psum x1 -> x0, waiting for transfers between devices: 274 us -> none  [on_device(): lax.psum((in_grad, out_grad, gain_grad), ('tm', 'rows', 'dp'))]
    psum x2 -> x0, blocking collectives: 196 us -> none  [the longest x1 114 us: on_device(): decay_grad = lax.psum(decay_part, ('rows', 'dp')) * decay_scale]
    pallas_call x0 -> x1, Pallas kernels: none -> 63.3 us  [on_device(): pl.pallas_call(functools.partial(body, nt, nz, nx, cells, cells * T * nt)...]
    all_gather x4 -> x0, blocking collectives: 46.9 us -> none  [the longest x2 24.6 us: prefix(): pieces = jax.tree.map(lambda part: lax.all_gather(part, axis), value)]
    dot_general x56 -> x0, matrix products: 38.6 us -> none  [the longest x18 11.8 us: kernel_grad(): lax.dot_general(piece, flat_grad, (((0,), (0,)), ((), ())), preferred_ele...]
    ppermute x8 -> x0, starting transfers between devices: 21.5 us -> none  [the longest x4 16.4 us: padded_2(): lax.ppermute(tail, axis, [(i, (i + 1) % count) for i in range(ends)])]
    convert_element_type x12 -> x0, other arithmetic: 9.1 us -> none  [the longest x8 5.52 us: entering_lap(): part[at].astype(own.dtype)]
    dot_general x2 -> x0, local copies, waits for them, and re-layouts: 7.45 us -> none  [the longest x1 3.72 us: on_device(): jnp.einsum('tkp,strcp->skrcp', within, state_grad, precision=lax.Precisio...]
  transfers between devices with their start and end apart: 9 -> 0, of which waited for: 1 -> 0; matrix products, arithmetic and copies ran while one was open for 2% -> 0% of each run, Pallas kernels for 0% -> 0%
where the time goes in v1:
time: 73.9 us; the launch traced here: 73.6 us
  Pallas kernels  63.3 us (86%)
  local copies, waits for them, and re-layouts  9.67 us (13%)
    pallas_call x1, Pallas kernels, on_device(): pl.pallas_call(functools.partial(body, nt, nz, nx, cells, cells * T * nt)...  63.3 us
    unnamed x18, local copies, waits for them, and re-layouts  9.67 us

profile of v1, /device:TPU:1, one launch (start us, length us, event | category | flops | bytes accessed | tf_op | source)
XLA Modules:
  0.0 73.6 jit_solution(9901009146891998158)
XLA Ops:
  0.6 0.0 copy-start.5
  0.6 0.6 copy-done.5
  1.3 0.0 copy-start
  1.3 1.0 %copy-done = bf16[1,16,4,32,128]{4,3,2,1,0:T(8,128)(2,1)S(1)} copy-done((bf16[1,16,4,32,128]{4,3,2,1,0:T(8,128)(2,1)S(1)}, bf16[1,16,4,32,128]{4,3,2,1,0:T(8,128)(2,1)}, u32[]{:S(2)}) %copy-start) | copy-done | bytes 524312
  2.3 0.0 copy-start.1
  2.3 1.0 %copy-done.1 = bf16[1,16,4,32,128]{4,3,2,1,0:T(8,128)(2,1)S(1)} copy-done((bf16[1,16,4,32,128]{4,3,2,1,0:T(8,128)(2,1)S(1)}, bf16[1,16,4,32,128]{4,3,2,1,0:T(8,128)(2,1)}, u32[]{:S(2)}) %copy-start.1) | copy-done | bytes 524312
  3.4 0.0 copy-start.2
  3.4 1.0 %copy-done.2 = bf16[3,3,128,128]{3,2,1,0:T(8,128)(2,1)S(1)} copy-done((bf16[3,3,128,128]{3,2,1,0:T(8,128)(2,1)S(1)}, bf16[3,3,128,128]{3,2,1,0:T(8,128)(2,1)}, u32[]{:S(2)}) %copy-start.2) | copy-done | bytes 294936
  4.3 0.0 copy-start.3
  4.3 1.0 %copy-done.3 = bf16[3,3,128,128]{3,2,1,0:T(8,128)(2,1)S(1)} copy-done((bf16[3,3,128,128]{3,2,1,0:T(8,128)(2,1)S(1)}, bf16[3,3,128,128]{3,2,1,0:T(8,128)(2,1)}, u32[]{:S(2)}) %copy-start.3) | copy-done | bytes 294936
  5.3 0.0 copy-start.4
  5.3 0.7 copy-done.4
  6.0 63.3 %shard_map.109 = (bf16[16,4,32,128]{3,2,1,0:T(8,128)(2,1)S(1)}, bf16[16,4,32,128]{3,2,1,0:T(8,128)(2,1)S(1)}, f32[3,3,128,128]{3,2,1,0:T(8,128)S(1)}, f32[3,3,12...) custom-call(bf16[16,4,32,128]{3,2,1,0:T(8,128)(2,1)S(1)} %bitcast.6, ...), custom_call_target="tpu_custom_call" | custom-call | tf_op jit(solution)/shard_map/pallas_call | solution.py:539
  69.3 0.8 %copy.18 = bf16[1,16,4,32,128]{4,3,2,1,0:T(8,128)(2,1)} copy(bf16[1,16,4,32,128]{4,3,2,1,0:T(8,128)(2,1)S(1)} %bitcast.9) | data formatting | bytes 1048576
  70.1 0.8 %copy.19 = bf16[1,16,4,32,128]{4,3,2,1,0:T(8,128)(2,1)} copy(bf16[1,16,4,32,128]{4,3,2,1,0:T(8,128)(2,1)S(1)} %bitcast.8) | data formatting | bytes 1048576
  70.9 0.8 %copy.20 = f32[3,3,128,128]{3,2,1,0:T(8,128)} copy(f32[3,3,128,128]{3,2,1,0:T(8,128)S(1)} %get-tuple-element.26) | data formatting | bytes 1179648
  71.7 0.8 %copy.21 = f32[3,3,128,128]{3,2,1,0:T(8,128)} copy(f32[3,3,128,128]{3,2,1,0:T(8,128)S(1)} %get-tuple-element.27) | data formatting | bytes 1179648
  72.5 0.5 copy.22
  73.0 0.6 copy.23
Async XLA Ops:
  0.6 0.7 copy-start.5
  1.3 1.0 %copy-start = (bf16[1,16,4,32,128]{4,3,2,1,0:T(8,128)(2,1)S(1)}, bf16[1,16,4,32,128]{4,3,2,1,0:T(8,128)(2,1)}, u32[]{:S(2)}) copy-start(bf16[1,16,4,32,128]{4,3,2,1,0:T(8,128)(2,1)} %param.6) | copy-start | bytes 1572868
  2.3 1.0 %copy-start.1 = (bf16[1,16,4,32,128]{4,3,2,1,0:T(8,128)(2,1)S(1)}, bf16[1,16,4,32,128]{4,3,2,1,0:T(8,128)(2,1)}, u32[]{:S(2)}) copy-start(bf16[1,16,4,32,128]{4,3,2,1,0:T(8,128)(2,1)} %param.7) | copy-start | bytes 1572868
  3.4 1.0 %copy-start.2 = (bf16[3,3,128,128]{3,2,1,0:T(8,128)(2,1)S(1)}, bf16[3,3,128,128]{3,2,1,0:T(8,128)(2,1)}, u32[]{:S(2)}) copy-start(bf16[3,3,128,128]{3,2,1,0:T(8,128)(2,1)} %w_in.1) | copy-start | bytes 884740
  4.3 1.0 %copy-start.3 = (bf16[3,3,128,128]{3,2,1,0:T(8,128)(2,1)S(1)}, bf16[3,3,128,128]{3,2,1,0:T(8,128)(2,1)}, u32[]{:S(2)}) copy-start(bf16[3,3,128,128]{3,2,1,0:T(8,128)(2,1)} %w_out.1) | copy-start | bytes 884740
  5.3 0.7 copy-start.4

commit v2 on v1

--- a/solution.py
+++ b/solution.py
@@ -15,6 +15,7 @@
 LANES = TAPS * C
 GELU_A = math.sqrt(2.0 / math.pi)
 GELU_B = 0.044715
+VMEM_BYTES = 59 * 10**6
 
 
 def at_next(field):
@@ -61,13 +62,13 @@
 
 def body(
     nt, nz, nx, total_cells, total_positions,
-    x_hbm, ct_hbm, w_in, w_out, gain, ld,
-    lo_hbm, vg_hbm, ig_out, og_out, gg_out, dg_out,
-    xpad, spad, g3, a3, st, ag, gp, ct, lo, vg,
+    x_hbm, ct_hbm, w_in_hbm, w_out_hbm, gain_hbm, ld_hbm,
+    lo_hbm, vg_hbm, g5_hbm, gg_hbm, dg_hbm,
+    xpad, spad, g3, a3, st, ag, gp, ct, w_in, w_out, gain, ld, lo, vg, gg_out, dg_out,
     es, eg, ea, hs, hg, ha, ces, cer,
     lam, ecum, erev, dsend, dall, csend, crecv, cin, bin_, gsum, dpart,
     acc, snd1, rcv1, snd2, rcv2, x3, f4, g5,
-    loc, hal_s, hal_r, ce_s, ce_r, dec_s, dec_r, car_s, car_r,
+    loc, out_s, hal_s, hal_r, ce_s, ce_r, dec_s, dec_r, car_s, car_r,
     p1_s, p1_r, p2_s, p2_r, p3_s, p3_r, p4_s, p4_r, p5_s, p5_r,
 ):
     T, R, W, _ = x_hbm.shape
@@ -110,10 +111,22 @@
                 barrier, inc=1, device_id={axis: k}, device_id_type=MESH
             ),
         )
-    load_x = pltpu.make_async_copy(x_hbm, xpad.at[:, 1 : R + 1], loc.at[0])
-    load_x.start()
-    load_ct = pltpu.make_async_copy(ct_hbm, ct, loc.at[1])
-    load_ct.start()
+    loads = [
+        pltpu.make_async_copy(src, dst, loc.at[n])
+        for n, (src, dst) in enumerate(
+            (
+                (ld_hbm, ld),
+                (x_hbm, xpad.at[:, 1 : R + 1]),
+                (w_in_hbm, w_in),
+                (ct_hbm, ct),
+                (w_out_hbm, w_out),
+                (gain_hbm, gain),
+            )
+        )
+    ]
+    for load in loads:
+        load.start()
+    loads[0].wait()
 
     run = jnp.zeros((1, C), F32)
     for t in range(T):
@@ -183,6 +196,11 @@
 
     others(me, nt, lambda k: decay_copy(k).start())
 
+    def store(n, src, dst):
+        copy = pltpu.make_async_copy(src, dst, out_s.at[n])
+        copy.start()
+        return copy
+
     def send1(q, k):
         return to_tm(snd1.at[q, k], rcv1.at[q, me], p1_s.at[q, k], p1_r.at[q, me], k)
 
@@ -259,16 +277,8 @@
         g5[q, me] = f4[q]
         others(me, nt, lambda k: send5(q, k).start())
 
-    weight_scale = 1.0 / math.sqrt(total_positions)
-
-    def sum6(q, out):
+    def sum6(q):
         others(me, nt, lambda k: got(g5, q, k, p5_r, to_tm))
-        for k in range(nt):
-            for u in range(0, CH, 16):
-                i, c = divmod(k * CH + u, C)
-                for j in range(TAPS):
-                    piece = g5[q, k, j * CH + u : j * CH + u + 16]
-                    out[i, j, c : c + 16] = piece.astype(F32) * weight_scale
 
     def sums_sent(q):
         others(me, nt, lambda k: send1(q, k).wait_send())
@@ -292,7 +302,8 @@
         y = forward_rows(xpad, w_in, frames, r0, nr)
         ag[frames, r0 : r0 + nr] = y.reshape(frames.size, nr, W, C)
 
-    load_x.wait()
+    loads[1].wait()
+    loads[2].wait()
     inner(drive)
     do_edges(0, "recv")
     outer(drive)
@@ -333,7 +344,8 @@
 
     each(0, T, finish_state)
 
-    load_ct.wait()
+    for load in loads[3:]:
+        load.wait()
 
     def output(frames, r0, nr):
         n = frames.size * nr
@@ -365,8 +377,6 @@
     eg[0] = gp[:, 0].astype(BF16)
     eg[1] = gp[:, R - 1].astype(BF16)
     do_edges(2, "start")
-    store_lo = pltpu.make_async_copy(lo, lo_hbm, loc.at[2])
-    store_lo.start()
 
     def kernel_grad(q, pad, wide):
         acc[q] = jnp.zeros((LANES, LANES), F32)
@@ -385,6 +395,7 @@
 
         each(0, 4, step)
 
+    store_lo = store(0, lo, lo_hbm)
     kernel_grad(0, spad, g3)
     sum1(0)
 
@@ -459,17 +470,19 @@
     sum3(1)
     sum5(0)
     outer(video_grad)
-    store_vg = pltpu.make_async_copy(vg, vg_hbm, loc.at[3])
-    store_vg.start()
+    store_vg = store(1, vg, vg_hbm)
     sum4(1)
-    sum6(0, og_out)
+    sum6(0)
+    store_og = store(2, g5.at[0], g5_hbm.at[0])
     sum5(1)
     dg_out[...] = f4[1, TAPS * CH : SR].astype(F32) * (1.0 / math.sqrt(total_cells))
     total_gain = jnp.zeros((8, C), F32)
     for k in range(nt):
         total_gain = total_gain + g5[0, k, TAPS * CH : SR].astype(F32)[0:8]
-    gg_out[...] = jnp.sum(total_gain, axis=0, keepdims=True) * weight_scale
-    sum6(1, ig_out)
+    gg_out[...] = jnp.sum(total_gain, axis=0, keepdims=True) * (1.0 / math.sqrt(total_positions))
+    store_small = (store(4, gg_out, gg_hbm), store(5, dg_out, dg_hbm))
+    sum6(1)
+    store_ig = store(3, g5.at[1], g5_hbm.at[1])
 
     for n in range(6):
         do_edges(n, "send")
@@ -478,8 +491,35 @@
     each(0, me, lambda k: carry_copy(1, k).wait_send())
     for q in range(2):
         sums_sent(q)
-    store_lo.wait()
-    store_vg.wait()
+    for copy in (store_lo, store_vg, store_og, store_ig, *store_small):
+        copy.wait()
+
+
+def finish(
+    scale, lo, vg, g5_hbm, gg, dg, lo_hbm, vg_hbm, ig_hbm, og_hbm, gg_hbm, dg_hbm, g5, grads, sems
+):
+    nt = g5.shape[1]
+    CH = LANES // nt
+
+    def store(n, src, dst):
+        copy = pltpu.make_async_copy(src, dst, sems.at[n])
+        copy.start()
+        return copy
+
+    load = store(6, g5_hbm, g5)
+    copies = [store(0, vg, vg_hbm), store(1, lo, lo_hbm)]
+    copies += [store(2, gg, gg_hbm), store(3, dg, dg_hbm)]
+    load.wait()
+    for q, out in ((0, og_hbm), (1, ig_hbm)):
+        for k in range(nt):
+            for u in range(0, CH, 16):
+                i, c = divmod(k * CH + u, C)
+                for j in range(TAPS):
+                    piece = g5[q, k, j * CH + u : j * CH + u + 16]
+                    grads[q, i, j, c : c + 16] = piece.astype(F32) * scale
+        copies.append(store(4 + q, grads.at[q], out))
+    for copy in copies:
+        copy.wait()
 
 
 def on_device(nt, nz, nx, video, cotangent, in_kernel, out_kernel, skip_gain, log_decay):
@@ -500,8 +540,14 @@
         vmem(field, F32),
         vmem(field, F32),
         vmem(field, BF16),
+        vmem((TAPS, TAPS, C, C), BF16),
+        vmem((TAPS, TAPS, C, C), BF16),
+        vmem((1, C), F32),
+        vmem((T, C), F32),
         vmem(field, BF16),
         vmem(field, BF16),
+        vmem((1, C), F32),
+        vmem((T, C), F32),
         *[vmem((2, T, W, C), BF16)] * 6,
         *[vmem((2, 2, W, C), BF16)] * 2,
         *[vmem((T, C), F32)] * 3,
@@ -521,7 +567,8 @@
         vmem((2, nx, BR, C), F32),
         vmem((2, NB * BR, C), BF16),
         vmem((2, nt, NB * BR, C), BF16),
-        dma((4,)),
+        dma((6,)),
+        dma((6,)),
         dma((4, 2)),
         dma((4, 2)),
         dma((2, 2)),
@@ -534,23 +581,22 @@
         *[dma((2, nz))] * 2,
         *[dma((2, nt))] * 2,
     ]
-    any_, whole = pl.BlockSpec(memory_space=pl.ANY), pl.BlockSpec(memory_space=pltpu.VMEM)
+    hbm = pl.BlockSpec(memory_space=pltpu.HBM)
     cells = seqs * nx * R * nz * W
-    outs = pl.pallas_call(
+    parts = pl.pallas_call(
         functools.partial(body, nt, nz, nx, cells, cells * T * nt),
         out_shape=(
             jax.ShapeDtypeStruct(field, BF16),
             jax.ShapeDtypeStruct(field, BF16),
-            jax.ShapeDtypeStruct((TAPS, TAPS, C, C), F32),
-            jax.ShapeDtypeStruct((TAPS, TAPS, C, C), F32),
+            jax.ShapeDtypeStruct((2, nt, NB * BR, C), BF16),
             jax.ShapeDtypeStruct((1, C), F32),
             jax.ShapeDtypeStruct((T, C), F32),
         ),
-        in_specs=[any_, any_, whole, whole, whole, whole],
-        out_specs=(any_, any_, whole, whole, whole, whole),
+        in_specs=[hbm] * 6,
+        out_specs=(hbm,) * 5,
         scratch_shapes=scratch,
         compiler_params=pltpu.CompilerParams(
-            collective_id=0, has_side_effects=True, vmem_limit_bytes=48 * 2**20
+            collective_id=0, has_side_effects=True, vmem_limit_bytes=VMEM_BYTES
         ),
     )(
         video.reshape(field),
@@ -560,6 +606,25 @@
         skip_gain.reshape(1, C),
         log_decay,
     )
+    outs = pl.pallas_call(
+        functools.partial(finish, 1.0 / math.sqrt(cells * T * nt)),
+        out_shape=(
+            jax.ShapeDtypeStruct(field, BF16),
+            jax.ShapeDtypeStruct(field, BF16),
+            jax.ShapeDtypeStruct((TAPS, TAPS, C, C), F32),
+            jax.ShapeDtypeStruct((TAPS, TAPS, C, C), F32),
+            jax.ShapeDtypeStruct((1, C), F32),
+            jax.ShapeDtypeStruct((T, C), F32),
+        ),
+        in_specs=[hbm] * 5,
+        out_specs=(hbm,) * 6,
+        scratch_shapes=[
+            vmem((2, nt, NB * BR, C), BF16),
+            vmem((2, TAPS, TAPS, C, C), F32),
+            dma((7,)),
+        ],
+        compiler_params=pltpu.CompilerParams(vmem_limit_bytes=VMEM_BYTES),
+    )(*parts)
     layer_out, video_grad, in_grad, out_grad, gain_grad, decay_grad = outs
     return (
         layer_out.reshape(video.shape),

time: 73.9 us -> 97.8 us (1.32)
  Pallas kernels: 63.3 us -> 97 us
  local copies, waits for them, and re-layouts: 9.67 us -> 0 us
    pallas_call x0 -> x1, Pallas kernels: none -> 33.2 us  [on_device(): pl.pallas_call(functools.partial(finish, 1.0 / math.sqrt(cells * T * nt))...]
    unnamed x18 -> x0, local copies, waits for them, and re-layouts: 9.67 us -> none
where the time goes in v2:
time: 97.8 us; the launch traced here: 97.7 us
  Pallas kernels  97 us (99%)
    pallas_call x1, Pallas kernels, on_device(): pl.pallas_call(functools.partial(body, nt, nz, nx, cells, cells * T * nt)...  63.9 us
    pallas_call x1, Pallas kernels, on_device(): pl.pallas_call(functools.partial(finish, 1.0 / math.sqrt(cells * T * nt))...  33.2 us

profile of v2, /device:TPU:1, one launch (start us, length us, event | category | flops | bytes accessed | tf_op | source)
XLA Modules:
  0.0 97.7 jit_solution(2341800491614171993)
XLA Ops:
  0.6 63.9 %shard_map.109 = (bf16[16,4,32,128]{3,2,1,0:T(8,128)(2,1)}, bf16[16,4,32,128]{3,2,1,0:T(8,128)(2,1)}, bf16[2,8,160,128]{3,2,1,0:T(8,128)(2,1)}, f32[1,128]{1,0:T(1,128)}, f32[16,128]{1,0:T(8,128)}) custom-call(bf16[16,4,32,128]{3,2,1,0:T(8,128)(2,1)} %bitcast.6, bf16[16,4,32,128]{3,2,1,0:T(8,128)(2,1)} %bitcast.7, bf16[3,3,128,128]{3,2,1,0:T(8,128)(2,1)} %w_in_hbm.1, ...), custom_call_target="tpu_custom_call" | custom-call | tf_op jit(solution)/shard_map/pallas_call | solution.py:586
  64.5 33.2 %shard_map.110 = (bf16[16,4,32,128]{3,2,1,0:T(8,128)(2,1)}, bf16[16,4,32,128]{3,2,1,0:T(8,128)(2,1)}, f32[3,3,128,128]{3,2,1,0:T(8,128)}, f32[3,3,128,128]{3,2,1...) custom-call(bf16[16,4,32,128]{3,2,1,0:T(8,128)(2,1)} %get-tuple-element.17.lo, ...), custom_call_target="tpu_custom_call" | custom-call | tf_op jit(solution)/shard_map/pallas_call | solution.py:609

commit v3 on v2

--- a/solution.py
+++ b/solution.py
@@ -15,7 +15,6 @@
 LANES = TAPS * C
 GELU_A = math.sqrt(2.0 / math.pi)
 GELU_B = 0.044715
-VMEM_BYTES = 59 * 10**6
 
 
 def at_next(field):
@@ -63,12 +62,12 @@
 def body(
     nt, nz, nx, total_cells, total_positions,
     x_hbm, ct_hbm, w_in_hbm, w_out_hbm, gain_hbm, ld_hbm,
-    lo_hbm, vg_hbm, g5_hbm, gg_hbm, dg_hbm,
-    xpad, spad, g3, a3, st, ag, gp, ct, w_in, w_out, gain, ld, lo, vg, gg_out, dg_out,
+    lo, vg, g5, gg_out, dg_out,
+    xpad, spad, g3, a3, st, ag, gp, ct, w_in, w_out, gain, ld,
     es, eg, ea, hs, hg, ha, ces, cer,
     lam, ecum, erev, dsend, dall, csend, crecv, cin, bin_, gsum, dpart,
-    acc, snd1, rcv1, snd2, rcv2, x3, f4, g5,
-    loc, out_s, hal_s, hal_r, ce_s, ce_r, dec_s, dec_r, car_s, car_r,
+    acc, snd1, rcv1, snd2, rcv2, x3, f4,
+    loc, hal_s, hal_r, ce_s, ce_r, dec_s, dec_r, car_s, car_r,
     p1_s, p1_r, p2_s, p2_r, p3_s, p3_r, p4_s, p4_r, p5_s, p5_r,
 ):
     T, R, W, _ = x_hbm.shape
@@ -196,11 +195,6 @@
 
     others(me, nt, lambda k: decay_copy(k).start())
 
-    def store(n, src, dst):
-        copy = pltpu.make_async_copy(src, dst, out_s.at[n])
-        copy.start()
-        return copy
-
     def send1(q, k):
         return to_tm(snd1.at[q, k], rcv1.at[q, me], p1_s.at[q, k], p1_r.at[q, me], k)
 
@@ -395,7 +389,6 @@
 
         each(0, 4, step)
 
-    store_lo = store(0, lo, lo_hbm)
     kernel_grad(0, spad, g3)
     sum1(0)
 
@@ -470,19 +463,15 @@
     sum3(1)
     sum5(0)
     outer(video_grad)
-    store_vg = store(1, vg, vg_hbm)
     sum4(1)
     sum6(0)
-    store_og = store(2, g5.at[0], g5_hbm.at[0])
     sum5(1)
     dg_out[...] = f4[1, TAPS * CH : SR].astype(F32) * (1.0 / math.sqrt(total_cells))
     total_gain = jnp.zeros((8, C), F32)
     for k in range(nt):
         total_gain = total_gain + g5[0, k, TAPS * CH : SR].astype(F32)[0:8]
     gg_out[...] = jnp.sum(total_gain, axis=0, keepdims=True) * (1.0 / math.sqrt(total_positions))
-    store_small = (store(4, gg_out, gg_hbm), store(5, dg_out, dg_hbm))
     sum6(1)
-    store_ig = store(3, g5.at[1], g5_hbm.at[1])
 
     for n in range(6):
         do_edges(n, "send")
@@ -491,13 +480,9 @@
     each(0, me, lambda k: carry_copy(1, k).wait_send())
     for q in range(2):
         sums_sent(q)
-    for copy in (store_lo, store_vg, store_og, store_ig, *store_small):
-        copy.wait()
-
-
-def finish(
-    scale, lo, vg, g5_hbm, gg, dg, lo_hbm, vg_hbm, ig_hbm, og_hbm, gg_hbm, dg_hbm, g5, grads, sems
-):
+
+
+def finish(scale, lo, vg, g5, gg, dg, lo_hbm, vg_hbm, ig_hbm, og_hbm, gg_hbm, dg_hbm, grads, sems):
     nt = g5.shape[1]
     CH = LANES // nt
 
@@ -506,10 +491,8 @@
         copy.start()
         return copy
 
-    load = store(6, g5_hbm, g5)
     copies = [store(0, vg, vg_hbm), store(1, lo, lo_hbm)]
     copies += [store(2, gg, gg_hbm), store(3, dg, dg_hbm)]
-    load.wait()
     for q, out in ((0, og_hbm), (1, ig_hbm)):
         for k in range(nt):
             for u in range(0, CH, 16):
@@ -544,10 +527,6 @@
         vmem((TAPS, TAPS, C, C), BF16),
         vmem((1, C), F32),
         vmem((T, C), F32),
-        vmem(field, BF16),
-        vmem(field, BF16),
-        vmem((1, C), F32),
-        vmem((T, C), F32),
         *[vmem((2, T, W, C), BF16)] * 6,
         *[vmem((2, 2, W, C), BF16)] * 2,
         *[vmem((T, C), F32)] * 3,
@@ -566,8 +545,6 @@
         vmem((2, nz, BR, C), BF16),
         vmem((2, nx, BR, C), F32),
         vmem((2, NB * BR, C), BF16),
-        vmem((2, nt, NB * BR, C), BF16),
-        dma((6,)),
         dma((6,)),
         dma((4, 2)),
         dma((4, 2)),
@@ -581,30 +558,35 @@
         *[dma((2, nz))] * 2,
         *[dma((2, nt))] * 2,
     ]
-    hbm = pl.BlockSpec(memory_space=pltpu.HBM)
+    hbm, whole = pl.BlockSpec(memory_space=pltpu.HBM), pl.BlockSpec(memory_space=pltpu.VMEM)
     cells = seqs * nx * R * nz * W
     parts = pl.pallas_call(
         functools.partial(body, nt, nz, nx, cells, cells * T * nt),
         out_shape=(
-            jax.ShapeDtypeStruct(field, BF16),
-            jax.ShapeDtypeStruct(field, BF16),
-            jax.ShapeDtypeStruct((2, nt, NB * BR, C), BF16),
-            jax.ShapeDtypeStruct((1, C), F32),
-            jax.ShapeDtypeStruct((T, C), F32),
+            vmem(field, BF16),
+            vmem(field, BF16),
+            vmem((2, nt, NB * BR, C), BF16),
+            vmem((1, C), F32),
+            vmem((T, C), F32),
         ),
         in_specs=[hbm] * 6,
-        out_specs=(hbm,) * 5,
+        out_specs=(whole,) * 5,
         scratch_shapes=scratch,
         compiler_params=pltpu.CompilerParams(
-            collective_id=0, has_side_effects=True, vmem_limit_bytes=VMEM_BYTES
+            collective_id=0, has_side_effects=True, vmem_limit_bytes=48 * 2**20
         ),
     )(
-        video.reshape(field),
-        cotangent.reshape(field),
-        in_kernel,
-        out_kernel,
-        skip_gain.reshape(1, C),
-        log_decay,
+        *[
+            pltpu.with_memory_space_constraint(operand, pltpu.HBM)
+            for operand in (
+                video.reshape(field),
+                cotangent.reshape(field),
+                in_kernel,
+                out_kernel,
+                skip_gain.reshape(1, C),
+                log_decay,
+            )
+        ]
     )
     outs = pl.pallas_call(
         functools.partial(finish, 1.0 / math.sqrt(cells * T * nt)),
@@ -616,14 +598,10 @@
             jax.ShapeDtypeStruct((1, C), F32),
             jax.ShapeDtypeStruct((T, C), F32),
         ),
-        in_specs=[hbm] * 5,
+        in_specs=[whole] * 5,
         out_specs=(hbm,) * 6,
-        scratch_shapes=[
-            vmem((2, nt, NB * BR, C), BF16),
-            vmem((2, TAPS, TAPS, C, C), F32),
-            dma((7,)),
-        ],
-        compiler_params=pltpu.CompilerParams(vmem_limit_bytes=VMEM_BYTES),
+        scratch_shapes=[vmem((2, TAPS, TAPS, C, C), F32), dma((6,))],
+        compiler_params=pltpu.CompilerParams(vmem_limit_bytes=16 * 2**20),
     )(*parts)
     layer_out, video_grad, in_grad, out_grad, gain_grad, decay_grad = outs
     return (

time: 97.8 us -> 65.9 us (0.67)
  Pallas kernels: 97 us -> 65.1 us
    pallas_call x1, Pallas kernels: 33.2 us -> 1.42 us  [on_device(): pl.pallas_call(functools.partial(finish, 1.0 / math.sqrt(cells * T * nt))...]
where the time goes in v3:
time: 65.9 us; the launch traced here: 65.8 us
  Pallas kernels  65.1 us (99%)
    pallas_call x1, Pallas kernels, on_device(): pl.pallas_call(functools.partial(body, nt, nz, nx, cells, cells * T * nt)...  63.7 us
    pallas_call x1, Pallas kernels, on_device(): pl.pallas_call(functools.partial(finish, 1.0 / math.sqrt(cells * T * nt))...  1.42 us

profile of v3, /device:TPU:1, one launch (start us, length us, event | category | flops | bytes accessed | tf_op | source)
XLA Modules:
  0.0 65.8 jit_solution(16650469212588345061)
XLA Ops:
  0.6 63.7 %shard_map.109 = (bf16[16,4,32,128]{3,2,1,0:T(8,128)(2,1)S(1)}, bf16[16,4,32,128]{3,2,1,0:T(8,128)(2,1)S(1)}, bf16[2,8,160,128]{3,2,1,0:T(8,128)(2,1)S(1)}, f32[1,128]{1,0:T(1,128)S(1)}, f32[16,128]{1,0:T(8,128)S(1)}) custom-call(bf16[16,4,32,128]{3,2,1,0:T(8,128)(2,1)} %bitcast.6, bf16[16,4,32,128]{3,2,1,0:T(8,128)(2,1)} %bitcast.7, ...), custom_call_target="tpu_custom_call" | custom-call | tf_op jit(solution)/shard_map/pallas_call | solution.py:563
  64.4 1.4 %shard_map.110 = (bf16[16,4,32,128]{3,2,1,0:T(8,128)(2,1)}, bf16[16,4,32,128]{3,2,1,0:T(8,128)(2,1)}, f32[3,3,128,128]{3,2,1,0:T(8,128)}, f32[3,3,128,128]{3,2,1...) custom-call(bf16[16,4,32,128]{3,2,1,0:T(8,128)(2,1)S(1)} %get-tuple-element.17.lo, ...), custom_call_target="tpu_custom_call" | custom-call | tf_op jit(solution)/shard_map/pallas_call | solution.py:591

commit v4 on v3

v4 whole, which is shorter than its diff:
```python
import functools
import math

import jax
import jax.numpy as jnp
from jax import lax
from jax.experimental import pallas as pl
from jax.experimental.pallas import tpu as pltpu
from jax.sharding import PartitionSpec as P

MESH = pl.DeviceIdType.MESH
F32, BF16 = jnp.float32, jnp.bfloat16
C = 128
TAPS = 3
LANES = TAPS * C
GELU_A = math.sqrt(2.0 / math.pi)
GELU_B = 0.044715


UNIT = 16
UNITS = LANES // UNIT


def share_of(nt, nx):
    return -(-(UNITS + 1) // (nt * nx)) * UNIT


def owners_of(grad, share):
    return -(-(UNITS + 1 - grad) * UNIT // share)


def at_next(field):
    cols = field.shape[1]
    col = lax.broadcasted_iota(jnp.int32, field.shape, 1)
    return jnp.where(col == cols - 1, 0.0, pltpu.roll(field, cols - 1, 1))


def at_previous(field):
    col = lax.broadcasted_iota(jnp.int32, field.shape, 1)
    return jnp.where(col == 0, 0.0, pltpu.roll(field, 1, 1))


def taps(w_ref, i):
    return jnp.concatenate([w_ref[i, j] for j in range(TAPS)], axis=-1)


def forward_rows(pad, w_ref, frames, r0, nr, which=range(TAPS)):
    n, cols = frames.size * nr, pad.shape[2]
    lhs = jnp.concatenate(
        [pad[frames, r0 + i : r0 + i + nr].reshape(n * cols, C) for i in which], axis=-1
    )
    rhs = jnp.concatenate([taps(w_ref, i) for i in which], axis=0)
    y = jnp.dot(lhs, rhs, preferred_element_type=F32).reshape(n, cols, LANES)
    return at_previous(y[..., :C]) + y[..., C : 2 * C] + at_next(y[..., 2 * C :])


def adjoint_rows(wide, w_ref, frames, r0, nr, which=range(TAPS)):
    n, cols = frames.size * nr, wide.shape[2]
    lhs = jnp.concatenate(
        [wide[frames, r0 + 2 - i : r0 + 2 - i + nr].reshape(n * cols, LANES) for i in which],
        axis=-1,
    )
    rhs = jnp.concatenate([taps(w_ref, i) for i in which], axis=-1)
    y = lax.dot_general(lhs, rhs, (((1,), (1,)), ((), ())), preferred_element_type=F32)
    return y.reshape(n, cols, C)


def widen(wide, frames, r0, nr, value):
    shape = (frames.size, nr) + value.shape[1:]
    for j, part in enumerate((at_next(value), value, at_previous(value))):
        wide[frames, r0 : r0 + nr, :, j * C : (j + 1) * C] = part.astype(BF16).reshape(shape)


def body(
    nt, nz, nx, total_cells, total_positions,
    x_hbm, ct_hbm, w_in_hbm, w_out_hbm, gain_hbm, ld_hbm,
    lo, vg, g5_0, g5_1, gg_out, dg_out,
    xpad, spad, g3, a3, st, ag, gp, ct, w_in, w_out, gain, ld,
    es, eg, ea, hs, hg, ha, ces, cer, nbs, nbr, nbd,
    lam, ecum, erev, dsend, dall, csend, crecv, cin, bin_, gsum, dpart,
    acc, loc, hal_s, hal_r, ce_s, ce_r, dec_s, dec_r, car_s, car_r,
    rcv1_0, rcv1_1, snd1_0, snd1_1, box_0, box_1, decays, sum_s, sum_r,
):
    T, R, W, _ = x_hbm.shape
    snd1, rcv1, box, g5 = (snd1_0, snd1_1), (rcv1_0, rcv1_1), (box_0, box_1), (g5_0, g5_1)
    group, share = nt * nx, rcv1_0.shape[1]
    owners = [owners_of(q, share) for q in range(2)]
    half = T // 2
    all_frames = pl.ds(0, T)
    me, mez, mex = lax.axis_index("tm"), lax.axis_index("rows"), lax.axis_index("dp")

    def to_tm(src, dst, s, r, k):
        return pltpu.make_async_remote_copy(src, dst, s, r, device_id={"tm": k}, device_id_type=MESH)

    def to_rows(src, dst, s, r, k):
        return pltpu.make_async_remote_copy(src, dst, s, r, device_id={"rows": k}, device_id_type=MESH)

    def to_dp(src, dst, s, r, k):
        return pltpu.make_async_remote_copy(src, dst, s, r, device_id={"dp": k}, device_id_type=MESH)

    def others(mine, count, act):
        def step(o, _):
            act(lax.rem(mine + o, count))
            return 0

        lax.fori_loop(1, count, step, 0)

    def each(low, high, act):
        def step(k, _):
            act(k)
            return 0

        lax.fori_loop(low, high, step, 0)

    barrier = pltpu.get_barrier_semaphore()
    mine = me * nx + mex

    def member(k):
        return {"tm": k // nx, "dp": lax.rem(k, nx)}

    def greet(place):
        pl.semaphore_signal(barrier, inc=1, device_id=place, device_id_type=MESH)

    others(mez, nz, lambda k: greet({"rows": k}))
    others(mine, group, lambda k: greet(member(k)))
    loads = [
        pltpu.make_async_copy(src, dst, loc.at[n])
        for n, (src, dst) in enumerate(
            (
                (ld_hbm, ld),
                (x_hbm, xpad.at[:, 1 : R + 1]),
                (w_in_hbm, w_in),
                (ct_hbm, ct),
                (w_out_hbm, w_out),
                (gain_hbm, gain),
            )
        )
    ]
    for load in loads:
        load.start()
    loads[0].wait()

    run = jnp.zeros((1, C), F32)
    for t in range(T):
        run = run + ld[t : t + 1]
        ecum[t : t + 1] = run
    erev[...] = jnp.exp(run - ecum[...])
    ecum[...] = jnp.exp(ecum[...])
    lam[...] = jnp.exp(ld[...])
    dsend[...] = jnp.broadcast_to(jnp.exp(run), dsend.shape)
    gsum[...] = jnp.zeros_like(gsum)

    @pl.when(mez == 0)
    def _():
        for ref in (xpad, spad, g3, a3):
            ref[:, 0] = jnp.zeros((T, W, ref.shape[3]), BF16)
        nbr[:, 1] = jnp.zeros((2, W, C), BF16)

    @pl.when(mez == nz - 1)
    def _():
        for ref in (xpad, spad, g3, a3):
            ref[:, R + 1] = jnp.zeros((T, W, ref.shape[3]), BF16)
        nbr[:, 0] = jnp.zeros((2, W, C), BF16)

    def inner(act):
        each(0, 2, lambda f: act(pl.ds(f * half, half), 1, R - 2))

    def outer(act):
        each(0, 1, lambda f: act(all_frames, 0, 1))
        each(0, 1, lambda f: act(all_frames, R - 1, 1))

    loads[1].wait()
    loads[2].wait()

    def own_part(rows_of, wide, w_ref, top, bottom):
        def some(frames, r0, nr, which=range(TAPS)):
            return rows_of(wide, w_ref, frames, r0, nr, which).reshape(frames.size, nr, W, C)

        def inner_rows(frames, r0, nr):
            ag[frames, r0 : r0 + nr] = some(frames, r0, nr)

        inner(inner_rows)
        ag[:, 0:1] = some(all_frames, 0, 1, top[1])
        ag[:, R - 1 : R] = some(all_frames, R - 1, 1, bottom[0])
        nbd[0] = some(all_frames, -1, 1, top[0]).reshape(T, W, C)
        nbd[1] = some(all_frames, R, 1, bottom[1]).reshape(T, W, C)

    own_part(forward_rows, xpad, w_in, ((2,), (1, 2)), ((0, 1), (0,)))

    def own_forward_step(t, carried):
        rate = lam[pl.ds(t, 1)]
        state = rate.reshape(1, 1, C) * carried[0] + ag[t]
        above, below = rate * carried[1] + nbd[0, t], rate * carried[2] + nbd[1, t]
        st[t + 1, 1 : R - 1] = state[1 : R - 1]
        es[0, t] = state[0].astype(BF16)
        es[1, t] = state[R - 1].astype(BF16)
        nbd[0, t] = above
        nbd[1, t] = below
        return state, above, below

    nothing = (jnp.zeros((R, W, C), F32), jnp.zeros((W, C), F32), jnp.zeros((W, C), F32))
    last, above, below = lax.fori_loop(0, T, own_forward_step, nothing)
    nbs[0, 0] = above.astype(BF16)
    nbs[0, 1] = below.astype(BF16)

    pl.semaphore_wait(barrier, nz + group - 2)

    def edge(stage, way, src, dst, sems=None):
        s, r = sems or (hal_s, hal_r)
        return to_rows(
            src, dst, s.at[stage, way], r.at[stage, way],
            jnp.maximum(mez - 1, 0) if way == 0 else jnp.minimum(mez + 1, nz - 1),
        )

    def edges(stage, srcs, dsts, what, sems=None):
        for way in range(2):
            from_there = (mez < nz - 1) if way == 0 else (mez > 0)
            to_there = (mez > 0) if way == 0 else (mez < nz - 1)

            @pl.when(from_there if what == "recv" else to_there)
            def _(way=way):
                copy = edge(stage, way, srcs[way], dsts[way], sems)
                {"start": copy.start, "recv": copy.wait_recv, "send": copy.wait_send}[what]()

    def received(act):
        @pl.when(mez < nz - 1)
        def _():
            act(0, R + 1)

        @pl.when(mez > 0)
        def _():
            act(1, 0)

    edge_sets = [
        (0, (x_hbm.at[:, 0], x_hbm.at[:, R - 1]), (xpad.at[:, R + 1], xpad.at[:, 0]), None),
        (1, (es.at[0], es.at[1]), (hs.at[0], hs.at[1]), None),
        (2, (eg.at[0], eg.at[1]), (hg.at[0], hg.at[1]), None),
        (3, (ea.at[0], ea.at[1]), (ha.at[0], ha.at[1]), None),
        (0, (ces.at[0, 0], ces.at[0, 1]), (cer.at[0, 0], cer.at[0, 1]), (ce_s, ce_r)),
        (1, (ces.at[1, 0], ces.at[1, 1]), (cer.at[1, 0], cer.at[1, 1]), (ce_s, ce_r)),
        (2, (nbs.at[0, 0], nbs.at[0, 1]), (nbr.at[0, 0], nbr.at[0, 1]), (ce_s, ce_r)),
        (3, (nbs.at[1, 0], nbs.at[1, 1]), (nbr.at[1, 0], nbr.at[1, 1]), (ce_s, ce_r)),
    ]

    def do_edges(n, what):
        stage, srcs, dsts, sems = edge_sets[n]
        edges(stage, srcs, dsts, what, sems)

    do_edges(6, "start")
    do_edges(0, "start")
    do_edges(1, "start")

    def with_neighbours(way, rows):
        return jnp.concatenate(
            [
                rows[:1] + nbr[way, 1].astype(F32)[None],
                rows[1 : R - 1],
                rows[R - 1 :] + nbr[way, 0].astype(F32)[None],
            ],
            axis=0,
        )

    def decay_copy(k):
        return to_tm(dsend, dall.at[me], dec_s.at[k], dec_r.at[me], k)

    others(me, nt, lambda k: decay_copy(k).start())

    def got(ref, q, k, r, copy):
        return copy(ref.at[q, k], ref.at[q, k], r.at[q, k], r.at[q, k], 0).wait_recv()

    def to_member(src, dst, n, q, k):
        return pltpu.make_async_remote_copy(
            src, dst, sum_s.at[n, q], sum_r.at[n, q], device_id=member(k), device_id_type=MESH
        )

    def send1(q, k):
        return to_member(snd1[q].at[k], rcv1[q].at[mine], 0, q, k)

    def send2(q, k):
        here = box[q].at[mez]
        return to_rows(here, here, sum_s.at[1, q], sum_r.at[1, q], k)

    def send3(q, k):
        here = g5[q].at[mine]
        return to_member(here, here, 2, q, k)

    def send_decay(k):
        here = decays.at[mex]
        return to_dp(here, here, sum_s.at[3, 0], sum_r.at[3, 0], k)

    def passed(n, q, ref, count, way):
        if count:
            whole = ref.at[pl.ds(0, count)]
            copy = to_member(whole, whole, n, q, 0)
            {"recv": copy.wait_recv, "send": copy.wait_send}[way]()

    def owning(q, own, other):
        pl.when(mine < owners[q])(own)
        if owners[q] < group:
            pl.when(mine >= owners[q])(other)

    def not_me(k, act):
        @pl.when(k != mine)
        def _():
            act(k)

    def sum1(q, extra=None):
        for k in range(owners[q]):
            r0 = k * share
            rows = min(share, LANES - r0)
            if rows > 0:
                snd1[q][k, 0:rows] = acc[q, r0 : r0 + rows].astype(BF16)
            if rows < share:
                snd1[q][k, max(rows, 0) :] = jnp.zeros((share - max(rows, 0), LANES), BF16)
        if extra is not None:
            k, r = divmod(LANES, share)
            snd1[q][k, r : r + UNIT, 0:C] = extra.astype(BF16)
        each(0, owners[q], lambda k: not_me(k, lambda k: send1(q, k).start()))

    def sum2(q):
        def own():
            rcv1[q][mine] = snd1[q][mine]
            passed(0, q, rcv1[q], group - 1, "recv")

            def step(k, total):
                return total + rcv1[q][k].astype(F32)

            total = lax.fori_loop(1, group, step, rcv1[q][0].astype(F32))
            for j in range(TAPS):
                part = total[:, j * C : (j + 1) * C].astype(BF16)
                box[q][mez, j * share : (j + 1) * share] = part

        def other():
            box[q][mez, 0 : TAPS * share] = jnp.zeros((TAPS * share, C), BF16)

        owning(q, own, other)
        if q == 1:
            passed(3, 0, decays, nx - 1, "recv")
            total = decays[0]
            for k in range(1, nx):
                total = total + decays[k]
            box[q][mez, TAPS * share :] = total.astype(BF16)
            others(mez, nz, lambda k: send2(q, k).start())
        else:
            owning(q, lambda: others(mez, nz, lambda k: send2(q, k).start()), lambda: None)

    def sum3(q):
        def total(r0, r1):
            value = box[q][0, r0:r1].astype(F32)
            for k in range(1, nz):
                value = value + box[q][k, r0:r1].astype(F32)
            return value

        if q == 1:
            passed(1, q, box[q], nz - 1, "recv")

        def own():
            if q == 0:
                passed(1, q, box[q], nz - 1, "recv")
            for j in range(TAPS):
                part = total(j * share, (j + 1) * share).astype(BF16)
                g5[q][mine, :, j * C : (j + 1) * C] = part
            others(mine, group, lambda k: send3(q, k).start())

        owning(q, own, lambda: None)
        if q == 1:
            dg_out[...] = total(TAPS * share, TAPS * share + T) * (1.0 / math.sqrt(total_cells))

    def sum4(q):
        owning(
            q,
            lambda: passed(2, q, g5[q], owners[q] - 1, "recv"),
            lambda: passed(2, q, g5[q], owners[q], "recv"),
        )

    def sums_sent():
        for q in range(2):
            owning(
                q,
                lambda q=q: passed(0, q, snd1[q], owners[q] - 1, "send"),
                lambda q=q: passed(0, q, snd1[q], owners[q], "send"),
            )
            owning(q, lambda q=q: passed(2, q, rcv1[q], group - 1, "send"), lambda: None)
        owning(0, lambda: passed(1, 0, box[0], nz - 1, "send"), lambda: None)
        passed(1, 1, box[1], nz - 1, "send")
        passed(3, 0, decays, nx - 1, "send")

    def carry_copy(way, k):
        return to_tm(csend.at[way], crecv.at[way, me], car_s.at[way, k], car_r.at[way, me], k)

    do_edges(6, "recv")
    csend[0] = with_neighbours(0, last).astype(BF16)
    each(me + 1, nt, lambda k: carry_copy(0, k).start())

    do_edges(0, "recv")

    def add_drive(way, row):
        r, tap = (R - 1, 2) if way == 0 else (0, 0)
        more = forward_rows(xpad, w_in, all_frames, r, 1, (tap,))
        ag[:, r : r + 1] += more.reshape(T, 1, W, C)

    received(add_drive)

    def forward_step(t, carried):
        rate = lam[pl.ds(t, 1)]
        top, bottom = rate * carried[0] + ag[t, 0], rate * carried[1] + ag[t, R - 1]
        st[t + 1, 0] = top
        st[t + 1, R - 1] = bottom
        return top, bottom

    lax.fori_loop(0, T, forward_step, nothing[1:])

    others(me, nt, lambda k: to_tm(dsend, dall.at[k], dec_s.at[k], dec_r.at[k], 0).wait_recv())

    def join_earlier(k, state):
        got(crecv, 0, k, car_r, to_tm)
        return dall[k, 0:1].reshape(1, 1, C) * state + crecv[0, k].astype(F32)

    carry = lax.fori_loop(0, me, join_earlier, jnp.zeros((R, W, C), F32))
    ces[0, 0] = carry[0].astype(BF16)
    ces[0, 1] = carry[R - 1].astype(BF16)
    do_edges(4, "start")
    st[0] = carry
    cin[...] = carry

    def finish_state(t):
        state = st[t + 1] + ecum[pl.ds(t, 1)].reshape(1, 1, C) * cin[...]
        st[t + 1] = state
        spad[t, 1 : R + 1] = state.astype(BF16)

    each(0, T, finish_state)

    for load in loads[3:]:
        load.wait()

    def output(frames, r0, nr):
        n = frames.size * nr
        x = xpad[frames, r0 + 1 : r0 + 1 + nr].reshape(n, W, C).astype(F32)
        pre = forward_rows(spad, w_out, frames, r0, nr) + gain[...].reshape(1, 1, C) * x
        square = pre * pre
        bend = jnp.tanh(GELU_A * (pre + GELU_B * (square * pre)))
        rise = 0.5 * (1.0 + bend)
        lo[frames, r0 : r0 + nr] = (pre * rise).astype(BF16).reshape(frames.size, nr, W, C)
        slope = rise + 0.5 * pre * (1.0 - bend * bend) * (GELU_A * (1.0 + 3.0 * GELU_B * square))
        grad = ct[frames, r0 : r0 + nr].reshape(n, W, C).astype(F32) * slope
        gp[frames, r0 : r0 + nr] = grad.reshape(frames.size, nr, W, C)
        gsum[...] += jnp.sum((grad * x).reshape(n * W // 8, 8, C), axis=0)
        widen(g3, frames, r0 + 1, nr, grad)

    inner(output)
    do_edges(1, "recv")
    do_edges(4, "recv")

    def state_edge(way, row):
        def step(t):
            value = hs[way, t].astype(F32) + nbd[1 - way, t]
            value = value + ecum[pl.ds(t, 1)] * cer[0, way].astype(F32)
            spad[t, row] = value.astype(BF16)

        each(0, T, step)

    received(state_edge)
    outer(output)
    eg[0] = gp[:, 0].astype(BF16)
    eg[1] = gp[:, R - 1].astype(BF16)
    def kernel_grad(q, pad, wide):
        acc[q] = jnp.zeros((LANES, LANES), F32)
        part = T // 4

        def step(f):
            frames = pl.ds(f * part, part)
            n = part * R * W
            lhs = jnp.concatenate(
                [pad[frames, i : i + R].reshape(n, C) for i in range(TAPS)], axis=-1
            )
            rhs = wide[frames, 1 : R + 1].reshape(n, LANES)
            acc[q] += lax.dot_general(
                lhs, rhs, (((0,), (0,)), ((), ())), preferred_element_type=F32
            )

        each(0, 4, step)

    own_part(adjoint_rows, g3, w_out, ((0,), (0, 1)), ((1, 2), (2,)))

    def own_backward_step(o, carried):
        t = T - 1 - o
        rate = lam[pl.ds(t, 1)]
        adjoint = ag[t] + carried[0]
        above, below = nbd[0, t] + carried[1], nbd[1, t] + carried[2]
        ag[t, 1 : R - 1] = adjoint[1 : R - 1]
        ea[0, t] = adjoint[0].astype(BF16)
        ea[1, t] = adjoint[R - 1].astype(BF16)
        nbd[0, t] = above
        nbd[1, t] = below
        return rate.reshape(1, 1, C) * adjoint, rate * above, rate * below

    first, above, below = lax.fori_loop(0, T, own_backward_step, nothing)
    nbs[1, 0] = above.astype(BF16)
    nbs[1, 1] = below.astype(BF16)
    do_edges(7, "start")
    do_edges(2, "start")
    do_edges(3, "start")
    kernel_grad(0, spad, g3)
    do_edges(7, "recv")
    csend[1] = with_neighbours(1, first).astype(BF16)
    each(0, me, lambda k: carry_copy(1, k).start())
    sum1(0, jnp.concatenate([gsum[...], jnp.zeros((8, C), F32)], axis=0))

    do_edges(2, "recv")

    def add_state_grad(way, row):
        widen(g3, all_frames, row, 1, hg[way].astype(F32))
        r, tap = (R - 1, 0) if way == 0 else (0, 2)
        more = adjoint_rows(g3, w_out, all_frames, r, 1, (tap,))
        ag[:, r : r + 1] += more.reshape(T, 1, W, C)

    received(add_state_grad)

    def backward_step(o, carried):
        t = T - 1 - o
        rate = lam[pl.ds(t, 1)]
        top, bottom = ag[t, 0] + carried[0], ag[t, R - 1] + carried[1]
        ag[t, 0] = top
        ag[t, R - 1] = bottom
        return rate * top, rate * bottom

    lax.fori_loop(0, T, backward_step, nothing[1:])

    def join_later(o, adjoint):
        k = nt - 1 - o
        got(crecv, 1, k, car_r, to_tm)
        return dall[k, 0:1].reshape(1, 1, C) * adjoint + crecv[1, k].astype(F32)

    back = lax.fori_loop(0, nt - 1 - me, join_later, jnp.zeros((R, W, C), F32))
    ces[1, 0] = back[0].astype(BF16)
    ces[1, 1] = back[R - 1].astype(BF16)
    do_edges(5, "start")
    bin_[...] = back

    def finish_adjoint(t):
        adjoint = ag[t] + erev[pl.ds(t, 1)].reshape(1, 1, C) * bin_[...]
        product = jnp.sum((adjoint * st[t]).reshape(R * W, C), axis=0, keepdims=True)
        dpart[pl.ds(t, 1)] = product * lam[pl.ds(t, 1)]
        for j, part in enumerate((at_next(adjoint), adjoint, at_previous(adjoint))):
            a3[t, 1 : R + 1, :, j * C : (j + 1) * C] = part.astype(BF16)

    each(0, T, finish_adjoint)
    kernel_grad(1, xpad, a3)
    sum1(1)
    decays[mex] = dpart[...]
    others(mex, nx, lambda k: send_decay(k).start())
    sum2(0)

    def video_grad(frames, r0, nr):
        skip = gain[...].reshape(1, 1, C) * gp[frames, r0 : r0 + nr].reshape(-1, W, C)
        value = adjoint_rows(a3, w_in, frames, r0, nr) + skip
        vg[frames, r0 : r0 + nr] = value.astype(BF16).reshape(frames.size, nr, W, C)

    inner(video_grad)
    do_edges(3, "recv")
    do_edges(5, "recv")

    def adjoint_edge(way, row):
        def step(t):
            value = ha[way, t].astype(F32) + nbd[1 - way, t]
            value = value + erev[pl.ds(t, 1)] * cer[1, way].astype(F32)
            widen(a3, pl.ds(t, 1), row, 1, value.reshape(1, W, C))

        each(0, T, step)

    received(adjoint_edge)
    outer(video_grad)
    sum3(0)
    sum2(1)
    sum4(0)
    k, r = divmod(LANES, share)
    total_gain = jnp.sum(g5[0][k, r : r + UNIT, 0:C].astype(F32), axis=0, keepdims=True)
    gg_out[...] = total_gain * (1.0 / math.sqrt(total_positions))
    sum3(1)
    sum4(1)

    for n in range(8):
        do_edges(n, "send")
    others(me, nt, lambda k: decay_copy(k).wait_send())
    each(me + 1, nt, lambda k: carry_copy(0, k).wait_send())
    each(0, me, lambda k: carry_copy(1, k).wait_send())
    sums_sent()


def finish(
    scale, lo, vg, g5_0, g5_1, gg, dg, lo_hbm, vg_hbm, ig_hbm, og_hbm, gg_hbm, dg_hbm, grads, sems
):
    def store(n, src, dst):
        copy = pltpu.make_async_copy(src, dst, sems.at[n])
        copy.start()
        return copy

    copies = [store(0, vg, vg_hbm), store(1, lo, lo_hbm)]
    copies += [store(2, gg, gg_hbm), store(3, dg, dg_hbm)]
    share = g5_0.shape[1]
    for q, g5, out in ((0, g5_0, og_hbm), (1, g5_1, ig_hbm)):
        for row in range(0, LANES, UNIT):
            k, r = divmod(row, share)
            i, c = divmod(row, C)
            for j in range(TAPS):
                piece = g5[k, r : r + UNIT, j * C : (j + 1) * C]
                grads[q, i, j, c : c + UNIT] = piece.astype(F32) * scale
        copies.append(store(4 + q, grads.at[q], out))
    for copy in copies:
        copy.wait()


def on_device(nt, nz, nx, video, cotangent, in_kernel, out_kernel, skip_gain, log_decay):
    seqs, T, R, W, _ = video.shape
    field = (T, R, W, C)
    share = share_of(nt, nx)
    owners = [owners_of(q, share) for q in range(2)]
    dma = pltpu.SemaphoreType.DMA
    vmem = pltpu.VMEM
    scratch = [
        vmem((T, R + 2, W, C), BF16),
        vmem((T, R + 2, W, C), BF16),
        vmem((T, R + 2, W, LANES), BF16),
        vmem((T, R + 2, W, LANES), BF16),
        vmem((T + 1, R, W, C), F32),
        vmem(field, F32),
        vmem(field, F32),
        vmem(field, BF16),
        vmem((TAPS, TAPS, C, C), BF16),
        vmem((TAPS, TAPS, C, C), BF16),
        vmem((1, C), F32),
        vmem((T, C), F32),
        *[vmem((2, T, W, C), BF16)] * 6,
        *[vmem((2, 2, W, C), BF16)] * 4,
        vmem((2, T, W, C), F32),
        *[vmem((T, C), F32)] * 3,
        vmem((8, C), F32),
        vmem((nt, 8, C), F32),
        vmem((2, R, W, C), BF16),
        vmem((2, nt, R, W, C), BF16),
        vmem((R, W, C), F32),
        vmem((R, W, C), F32),
        vmem((8, C), F32),
        vmem((T, C), F32),
        vmem((2, LANES, LANES), F32),
        dma((6,)),
        dma((4, 2)),
        dma((4, 2)),
        dma((4, 2)),
        dma((4, 2)),
        dma((nt,)),
        dma((nt,)),
        *[dma((2, nt))] * 2,
    ]
    scratch += [vmem((nt * nx, share, LANES), BF16)] * 2
    scratch += [vmem((n, share, LANES), BF16) for n in owners]
    scratch += [vmem((nz, TAPS * share, C), BF16), vmem((nz, TAPS * share + T, C), BF16)]
    scratch += [vmem((nx, T, C), F32), dma((4, 2)), dma((4, 2))]
    hbm, whole = pl.BlockSpec(memory_space=pltpu.HBM), pl.BlockSpec(memory_space=pltpu.VMEM)
    cells = seqs * nx * R * nz * W
    pieces = pl.pallas_call(
        functools.partial(body, nt, nz, nx, cells, cells * T * nt),
        out_shape=(
            vmem(field, BF16),
            vmem(field, BF16),
            *[vmem((n, share, LANES), BF16) for n in owners],
            vmem((1, C), F32),
            vmem((T, C), F32),
        ),
        in_specs=[hbm] * 6,
        out_specs=(whole,) * 6,
        scratch_shapes=scratch,
        compiler_params=pltpu.CompilerParams(
            collective_id=0, has_side_effects=True, vmem_limit_bytes=48 * 2**20
        ),
    )(
        *[
            pltpu.with_memory_space_constraint(operand, pltpu.HBM)
            for operand in (
                video.reshape(field),
                cotangent.reshape(field),
                in_kernel,
                out_kernel,
                skip_gain.reshape(1, C),
                log_decay,
            )
        ]
    )
    outs = pl.pallas_call(
        functools.partial(finish, 1.0 / math.sqrt(cells * T * nt)),
        out_shape=(
            jax.ShapeDtypeStruct(field, BF16),
            jax.ShapeDtypeStruct(field, BF16),
            jax.ShapeDtypeStruct((TAPS, TAPS, C, C), F32),
            jax.ShapeDtypeStruct((TAPS, TAPS, C, C), F32),
            jax.ShapeDtypeStruct((1, C), F32),
            jax.ShapeDtypeStruct((T, C), F32),
        ),
        in_specs=[whole] * 6,
        out_specs=(hbm,) * 6,
        scratch_shapes=[vmem((2, TAPS, TAPS, C, C), F32), dma((6,))],
        compiler_params=pltpu.CompilerParams(vmem_limit_bytes=16 * 2**20),
    )(*pieces)
    layer_out, video_grad, in_grad, out_grad, gain_grad, decay_grad = outs
    return (
        layer_out.reshape(video.shape),
        video_grad.reshape(video.shape),
        in_grad,
        out_grad,
        gain_grad.reshape(C),
        decay_grad,
    )


def solution(mesh):
    field = P("dp", "tm", "rows", None, None)
    nt, nz, nx = mesh.shape["tm"], mesh.shape["rows"], mesh.shape["dp"]
    return jax.shard_map(
        functools.partial(on_device, nt, nz, nx),
        mesh=mesh,
        in_specs=(field, field, P(), P(), P(), P("tm", None)),
        out_specs=(field, field, P(), P(), P(), P("tm", None)),
        check_vma=False,
    )
```

time: 65.9 us -> 62.5 us (0.948)
  Pallas kernels: 65.1 us -> 61.8 us
    pallas_call x1, Pallas kernels: 63.7 us -> 60.4 us  [on_device(): pl.pallas_call(functools.partial(body, nt, nz, nx, cells, cells * T * nt)...]
where the time goes in v4:
time: 62.5 us; the launch traced here: 62.4 us
  Pallas kernels  61.8 us (99%)
  between operations  0.64 us (1%)
    pallas_call x1, Pallas kernels, on_device(): pl.pallas_call(functools.partial(body, nt, nz, nx, cells, cells * T * nt)...  60.4 us
    pallas_call x1, Pallas kernels, on_device(): pl.pallas_call(functools.partial(finish, 1.0 / math.sqrt(cells * T * nt))...  1.42 us

profile of v4, /device:TPU:1, one launch (start us, length us, event | category | flops | bytes accessed | tf_op | source)
XLA Modules:
  0.0 62.4 jit_solution(9722791617159916794)
XLA Ops:
  0.6 60.4 %shard_map.109 = (bf16[16,4,32,128]{3,2,1,0:T(8,128)(2,1)S(1)}, bf16[16,4,32,128]{3,2,1,0:T(8,128)(2,1)S(1)}, bf16[25,16,384]{2,1,0:T(8,128)(2,1)S(1)}, bf16[24,...) custom-call(bf16[16,4,32,128]{3,2,1,0:T(8,128)(2,1)} %bitcast.6, ...), custom_call_target="tpu_custom_call" | custom-call | tf_op jit(solution)/shard_map/pallas_call | solution.py:661
  61.0 1.4 %shard_map.110 = (bf16[16,4,32,128]{3,2,1,0:T(8,128)(2,1)}, bf16[16,4,32,128]{3,2,1,0:T(8,128)(2,1)}, f32[3,3,128,128]{3,2,1,0:T(8,128)}, f32[3,3,128,128]{3,2,1...) custom-call(bf16[16,4,32,128]{3,2,1,0:T(8,128)(2,1)S(1)} %get-tuple-element.18.lo, ...), custom_call_target="tpu_custom_call" | custom-call | tf_op jit(solution)/shard_map/pallas_call | solution.py:689

commit v5 on v4

--- a/solution.py
+++ b/solution.py
@@ -79,7 +79,7 @@
     es, eg, ea, hs, hg, ha, ces, cer, nbs, nbr, nbd,
     lam, ecum, erev, dsend, dall, csend, crecv, cin, bin_, gsum, dpart,
     acc, loc, hal_s, hal_r, ce_s, ce_r, dec_s, dec_r, car_s, car_r,
-    rcv1_0, rcv1_1, snd1_0, snd1_1, box_0, box_1, decays, sum_s, sum_r,
+    rcv1_0, rcv1_1, snd1_0, snd1_1, box_0, box_1, decays, dbox, sum_s, sum_r,
 ):
     T, R, W, _ = x_hbm.shape
     snd1, rcv1, box, g5 = (snd1_0, snd1_1), (rcv1_0, rcv1_1), (box_0, box_1), (g5_0, g5_1)
@@ -288,6 +288,10 @@
         here = decays.at[mex]
         return to_dp(here, here, sum_s.at[3, 0], sum_r.at[3, 0], k)
 
+    def send_decay_band(k):
+        here = dbox.at[mez]
+        return to_rows(here, here, sum_s.at[3, 1], sum_r.at[3, 1], k)
+
     def passed(n, q, ref, count, way):
         if count:
             whole = ref.at[pl.ds(0, count)]
@@ -330,41 +334,41 @@
                 part = total[:, j * C : (j + 1) * C].astype(BF16)
                 box[q][mez, j * share : (j + 1) * share] = part
 
-        def other():
-            box[q][mez, 0 : TAPS * share] = jnp.zeros((TAPS * share, C), BF16)
-
-        owning(q, own, other)
-        if q == 1:
-            passed(3, 0, decays, nx - 1, "recv")
-            total = decays[0]
-            for k in range(1, nx):
-                total = total + decays[k]
-            box[q][mez, TAPS * share :] = total.astype(BF16)
             others(mez, nz, lambda k: send2(q, k).start())
-        else:
-            owning(q, lambda: others(mez, nz, lambda k: send2(q, k).start()), lambda: None)
+
+        owning(q, own, lambda: None)
 
     def sum3(q):
-        def total(r0, r1):
-            value = box[q][0, r0:r1].astype(F32)
+        def own():
+            passed(1, q, box[q], nz - 1, "recv")
+            total = box[q][0].astype(F32)
             for k in range(1, nz):
-                value = value + box[q][k, r0:r1].astype(F32)
-            return value
-
-        if q == 1:
-            passed(1, q, box[q], nz - 1, "recv")
-
-        def own():
-            if q == 0:
-                passed(1, q, box[q], nz - 1, "recv")
+                total = total + box[q][k].astype(F32)
             for j in range(TAPS):
-                part = total(j * share, (j + 1) * share).astype(BF16)
+                part = total[j * share : (j + 1) * share].astype(BF16)
                 g5[q][mine, :, j * C : (j + 1) * C] = part
             others(mine, group, lambda k: send3(q, k).start())
 
         owning(q, own, lambda: None)
-        if q == 1:
-            dg_out[...] = total(TAPS * share, TAPS * share + T) * (1.0 / math.sqrt(total_cells))
+
+    def decay1():
+        decays[mex] = dpart[...]
+        others(mex, nx, lambda k: send_decay(k).start())
+
+    def decay2():
+        passed(3, 0, decays, nx - 1, "recv")
+        total = decays[0]
+        for k in range(1, nx):
+            total = total + decays[k]
+        dbox[mez] = total.astype(BF16)
+        others(mez, nz, lambda k: send_decay_band(k).start())
+
+    def decay3():
+        passed(3, 1, dbox, nz - 1, "recv")
+        total = dbox[0].astype(F32)
+        for k in range(1, nz):
+            total = total + dbox[k].astype(F32)
+        dg_out[...] = total * (1.0 / math.sqrt(total_cells))
 
     def sum4(q):
         owning(
@@ -381,8 +385,8 @@
                 lambda q=q: passed(0, q, snd1[q], owners[q], "send"),
             )
             owning(q, lambda q=q: passed(2, q, rcv1[q], group - 1, "send"), lambda: None)
-        owning(0, lambda: passed(1, 0, box[0], nz - 1, "send"), lambda: None)
-        passed(1, 1, box[1], nz - 1, "send")
+            owning(q, lambda q=q: passed(1, q, box[q], nz - 1, "send"), lambda: None)
+        passed(3, 1, dbox, nz - 1, "send")
         passed(3, 0, decays, nx - 1, "send")
 
     def carry_copy(way, k):
@@ -547,8 +551,7 @@
     each(0, T, finish_adjoint)
     kernel_grad(1, xpad, a3)
     sum1(1)
-    decays[mex] = dpart[...]
-    others(mex, nx, lambda k: send_decay(k).start())
+    decay1()
     sum2(0)
 
     def video_grad(frames, r0, nr):
@@ -570,13 +573,15 @@
 
     received(adjoint_edge)
     outer(video_grad)
+    sum2(1)
+    decay2()
     sum3(0)
-    sum2(1)
+    sum3(1)
     sum4(0)
     k, r = divmod(LANES, share)
     total_gain = jnp.sum(g5[0][k, r : r + UNIT, 0:C].astype(F32), axis=0, keepdims=True)
     gg_out[...] = total_gain * (1.0 / math.sqrt(total_positions))
-    sum3(1)
+    decay3()
     sum4(1)
 
     for n in range(8):
@@ -654,8 +659,8 @@
     ]
     scratch += [vmem((nt * nx, share, LANES), BF16)] * 2
     scratch += [vmem((n, share, LANES), BF16) for n in owners]
-    scratch += [vmem((nz, TAPS * share, C), BF16), vmem((nz, TAPS * share + T, C), BF16)]
-    scratch += [vmem((nx, T, C), F32), dma((4, 2)), dma((4, 2))]
+    scratch += [vmem((nz, TAPS * share, C), BF16)] * 2
+    scratch += [vmem((nx, T, C), F32), vmem((nz, T, C), BF16), dma((4, 2)), dma((4, 2))]
     hbm, whole = pl.BlockSpec(memory_space=pltpu.HBM), pl.BlockSpec(memory_space=pltpu.VMEM)
     cells = seqs * nx * R * nz * W
     pieces = pl.pallas_call(

time: 62.5 us -> 61.4 us (0.982)
  Pallas kernels: 61.8 us -> 60.6 us
    pallas_call x1, Pallas kernels: 60.4 us -> 59.2 us  [on_device(): pl.pallas_call(functools.partial(body, nt, nz, nx, cells, cells * T * nt)...]
where the time goes in v5:
time: 61.4 us; the launch traced here: 61.2 us
  Pallas kernels  60.6 us (99%)
  between operations  0.64 us (1%)
    pallas_call x1, Pallas kernels, on_device(): pl.pallas_call(functools.partial(body, nt, nz, nx, cells, cells * T * nt)...  59.2 us
    pallas_call x1, Pallas kernels, on_device(): pl.pallas_call(functools.partial(finish, 1.0 / math.sqrt(cells * T * nt))...  1.42 us

profile of v5, /device:TPU:1, one launch (start us, length us, event | category | flops | bytes accessed | tf_op | source)
XLA Modules:
  0.0 61.2 jit_solution(17414254147201273203)
XLA Ops:
  0.6 59.2 %shard_map.109 = (bf16[16,4,32,128]{3,2,1,0:T(8,128)(2,1)S(1)}, bf16[16,4,32,128]{3,2,1,0:T(8,128)(2,1)S(1)}, bf16[25,16,384]{2,1,0:T(8,128)(2,1)S(1)}, bf16[24,...) custom-call(bf16[16,4,32,128]{3,2,1,0:T(8,128)(2,1)} %bitcast.6, ...), custom_call_target="tpu_custom_call" | custom-call | tf_op jit(solution)/shard_map/pallas_call | solution.py:666
  59.8 1.4 %shard_map.110 = (bf16[16,4,32,128]{3,2,1,0:T(8,128)(2,1)}, bf16[16,4,32,128]{3,2,1,0:T(8,128)(2,1)}, f32[3,3,128,128]{3,2,1,0:T(8,128)}, f32[3,3,128,128]{3,2,1...) custom-call(bf16[16,4,32,128]{3,2,1,0:T(8,128)(2,1)S(1)} %get-tuple-element.18.lo, ...), custom_call_target="tpu_custom_call" | custom-call | tf_op jit(solution)/shard_map/pallas_call | solution.py:694

commit v6 on v5

--- a/solution.py
+++ b/solution.py
@@ -172,20 +172,24 @@
     loads[1].wait()
     loads[2].wait()
 
-    def own_part(rows_of, wide, w_ref, top, bottom):
-        def some(frames, r0, nr, which=range(TAPS)):
-            return rows_of(wide, w_ref, frames, r0, nr, which).reshape(frames.size, nr, W, C)
-
+    def some_rows(rows_of, wide, w_ref, frames, r0, nr, which=range(TAPS)):
+        return rows_of(wide, w_ref, frames, r0, nr, which).reshape(frames.size, nr, W, C)
+
+    def own_rows(rows_of, wide, w_ref, top, bottom):
         def inner_rows(frames, r0, nr):
-            ag[frames, r0 : r0 + nr] = some(frames, r0, nr)
+            ag[frames, r0 : r0 + nr] = some_rows(rows_of, wide, w_ref, frames, r0, nr)
 
         inner(inner_rows)
-        ag[:, 0:1] = some(all_frames, 0, 1, top[1])
-        ag[:, R - 1 : R] = some(all_frames, R - 1, 1, bottom[0])
-        nbd[0] = some(all_frames, -1, 1, top[0]).reshape(T, W, C)
-        nbd[1] = some(all_frames, R, 1, bottom[1]).reshape(T, W, C)
-
-    own_part(forward_rows, xpad, w_in, ((2,), (1, 2)), ((0, 1), (0,)))
+        ag[:, 0:1] = some_rows(rows_of, wide, w_ref, all_frames, 0, 1, top)
+        ag[:, R - 1 : R] = some_rows(rows_of, wide, w_ref, all_frames, R - 1, 1, bottom)
+
+    def next_rows(rows_of, wide, w_ref, above, below):
+        for n, (r0, tap) in enumerate(((-1, above), (R, below))):
+            part = some_rows(rows_of, wide, w_ref, all_frames, r0, 1, (tap,))
+            nbd[n] = part.reshape(T, W, C)
+
+    own_rows(forward_rows, xpad, w_in, (1, 2), (0, 1))
+    next_rows(forward_rows, xpad, w_in, 2, 0)
 
     def own_forward_step(t, carried):
         rate = lam[pl.ds(t, 1)]
@@ -302,11 +306,6 @@
         pl.when(mine < owners[q])(own)
         if owners[q] < group:
             pl.when(mine >= owners[q])(other)
-
-    def not_me(k, act):
-        @pl.when(k != mine)
-        def _():
-            act(k)
 
     def sum1(q, extra=None):
         for k in range(owners[q]):
@@ -319,7 +318,12 @@
         if extra is not None:
             k, r = divmod(LANES, share)
             snd1[q][k, r : r + UNIT, 0:C] = extra.astype(BF16)
-        each(0, owners[q], lambda k: not_me(k, lambda k: send1(q, k).start()))
+        def to_owner(k):
+            @pl.when(k < owners[q])
+            def _():
+                send1(q, k).start()
+
+        others(mine, group, to_owner)
 
     def sum2(q):
         def own():
@@ -484,31 +488,38 @@
 
         each(0, 4, step)
 
-    own_part(adjoint_rows, g3, w_out, ((0,), (0, 1)), ((1, 2), (2,)))
-
-    def own_backward_step(o, carried):
+    next_rows(adjoint_rows, g3, w_out, 0, 2)
+
+    def next_backward_step(o, carried):
         t = T - 1 - o
         rate = lam[pl.ds(t, 1)]
-        adjoint = ag[t] + carried[0]
-        above, below = nbd[0, t] + carried[1], nbd[1, t] + carried[2]
-        ag[t, 1 : R - 1] = adjoint[1 : R - 1]
-        ea[0, t] = adjoint[0].astype(BF16)
-        ea[1, t] = adjoint[R - 1].astype(BF16)
+        above, below = nbd[0, t] + carried[0], nbd[1, t] + carried[1]
         nbd[0, t] = above
         nbd[1, t] = below
-        return rate.reshape(1, 1, C) * adjoint, rate * above, rate * below
-
-    first, above, below = lax.fori_loop(0, T, own_backward_step, nothing)
+        return rate * above, rate * below
+
+    above, below = lax.fori_loop(0, T, next_backward_step, nothing[1:])
     nbs[1, 0] = above.astype(BF16)
     nbs[1, 1] = below.astype(BF16)
     do_edges(7, "start")
     do_edges(2, "start")
-    do_edges(3, "start")
-    kernel_grad(0, spad, g3)
+
+    own_rows(adjoint_rows, g3, w_out, (0, 1), (1, 2))
+
+    def own_backward_step(o, carried):
+        t = T - 1 - o
+        adjoint = ag[t] + carried
+        ag[t, 1 : R - 1] = adjoint[1 : R - 1]
+        ea[0, t] = adjoint[0].astype(BF16)
+        ea[1, t] = adjoint[R - 1].astype(BF16)
+        return lam[pl.ds(t, 1)].reshape(1, 1, C) * adjoint
+
+    first = lax.fori_loop(0, T, own_backward_step, nothing[0])
     do_edges(7, "recv")
     csend[1] = with_neighbours(1, first).astype(BF16)
     each(0, me, lambda k: carry_copy(1, k).start())
-    sum1(0, jnp.concatenate([gsum[...], jnp.zeros((8, C), F32)], axis=0))
+    do_edges(3, "start")
+    kernel_grad(0, spad, g3)
 
     do_edges(2, "recv")
 
@@ -529,6 +540,7 @@
         return rate * top, rate * bottom
 
     lax.fori_loop(0, T, backward_step, nothing[1:])
+    sum1(0, jnp.concatenate([gsum[...], jnp.zeros((8, C), F32)], axis=0))
 
     def join_later(o, adjoint):
         k = nt - 1 - o

time: 61.4 us -> 61 us (level)
  no operation moved by 1% of the time
where the time goes in v6:
time: 61 us; the launch traced here: 60.9 us
  Pallas kernels  60.2 us (99%)
  between operations  0.64 us (1%)
    pallas_call x1, Pallas kernels, on_device(): pl.pallas_call(functools.partial(body, nt, nz, nx, cells, cells * T * nt)...  58.8 us
    pallas_call x1, Pallas kernels, on_device(): pl.pallas_call(functools.partial(finish, 1.0 / math.sqrt(cells * T * nt))...  1.42 us

profile of v6, /device:TPU:1, one launch (start us, length us, event | category | flops | bytes accessed | tf_op | source)
XLA Modules:
  0.0 60.9 jit_solution(11074458638110072815)
XLA Ops:
  0.6 58.8 %shard_map.109 = (bf16[16,4,32,128]{3,2,1,0:T(8,128)(2,1)S(1)}, bf16[16,4,32,128]{3,2,1,0:T(8,128)(2,1)S(1)}, bf16[25,16,384]{2,1,0:T(8,128)(2,1)S(1)}, bf16[24,...) custom-call(bf16[16,4,32,128]{3,2,1,0:T(8,128)(2,1)} %bitcast.6, ...), custom_call_target="tpu_custom_call" | custom-call | tf_op jit(solution)/shard_map/pallas_call | solution.py:678
  59.4 1.4 %shard_map.110 = (bf16[16,4,32,128]{3,2,1,0:T(8,128)(2,1)}, bf16[16,4,32,128]{3,2,1,0:T(8,128)(2,1)}, f32[3,3,128,128]{3,2,1,0:T(8,128)}, f32[3,3,128,128]{3,2,1...) custom-call(bf16[16,4,32,128]{3,2,1,0:T(8,128)(2,1)S(1)} %get-tuple-element.18.lo, ...), custom_call_target="tpu_custom_call" | custom-call | tf_op jit(solution)/shard_map/pallas_call | solution.py:706

commit v7 on v6

--- a/solution.py
+++ b/solution.py
@@ -561,9 +561,9 @@
             a3[t, 1 : R + 1, :, j * C : (j + 1) * C] = part.astype(BF16)
 
     each(0, T, finish_adjoint)
+    decay1()
     kernel_grad(1, xpad, a3)
     sum1(1)
-    decay1()
     sum2(0)
 
     def video_grad(frames, r0, nr):
@@ -572,6 +572,7 @@
         vg[frames, r0 : r0 + nr] = value.astype(BF16).reshape(frames.size, nr, W, C)
 
     inner(video_grad)
+    decay2()
     do_edges(3, "recv")
     do_edges(5, "recv")
 
@@ -586,14 +587,13 @@
     received(adjoint_edge)
     outer(video_grad)
     sum2(1)
-    decay2()
     sum3(0)
+    decay3()
     sum3(1)
     sum4(0)
     k, r = divmod(LANES, share)
     total_gain = jnp.sum(g5[0][k, r : r + UNIT, 0:C].astype(F32), axis=0, keepdims=True)
     gg_out[...] = total_gain * (1.0 / math.sqrt(total_positions))
-    decay3()
     sum4(1)
 
     for n in range(8):

time: 61 us -> 60.9 us (level)
  no operation moved by 1% of the time
where the time goes in v7:
time: 60.9 us; the launch traced here: 60.7 us
  Pallas kernels  60.1 us (99%)
  between operations  0.64 us (1%)
    pallas_call x1, Pallas kernels, on_device(): pl.pallas_call(functools.partial(body, nt, nz, nx, cells, cells * T * nt)...  58.7 us
    pallas_call x1, Pallas kernels, on_device(): pl.pallas_call(functools.partial(finish, 1.0 / math.sqrt(cells * T * nt))...  1.42 us

profile of v7, /device:TPU:1, one launch (start us, length us, event | category | flops | bytes accessed | tf_op | source)
XLA Modules:
  0.0 60.7 jit_solution(6349429907743094604)
XLA Ops:
  0.6 58.7 %shard_map.109 = (bf16[16,4,32,128]{3,2,1,0:T(8,128)(2,1)S(1)}, bf16[16,4,32,128]{3,2,1,0:T(8,128)(2,1)S(1)}, bf16[25,16,384]{2,1,0:T(8,128)(2,1)S(1)}, bf16[24,...) custom-call(bf16[16,4,32,128]{3,2,1,0:T(8,128)(2,1)} %bitcast.6, ...), custom_call_target="tpu_custom_call" | custom-call | tf_op jit(solution)/shard_map/pallas_call | solution.py:678
  59.3 1.4 %shard_map.110 = (bf16[16,4,32,128]{3,2,1,0:T(8,128)(2,1)}, bf16[16,4,32,128]{3,2,1,0:T(8,128)(2,1)}, f32[3,3,128,128]{3,2,1,0:T(8,128)}, f32[3,3,128,128]{3,2,1...) custom-call(bf16[16,4,32,128]{3,2,1,0:T(8,128)(2,1)S(1)} %get-tuple-element.18.lo, ...), custom_call_target="tpu_custom_call" | custom-call | tf_op jit(solution)/shard_map/pallas_call | solution.py:706
